TPU v7x, 256 devices: a whole 4x4x8 slice. The times are simulated.
256 devices in a mesh: seq: 64 (over z, x, core), head: 4 (over y).
Axes of the slice: x: 4, y: 4, z: 8, core: 2. Of those that a mesh axis runs over, the one named last changes fastest.
Arguments:
- x_in: bfloat16 [24576, 8192], P('seq', 'head'), may hold values from -6 to 6
- bc_in: bfloat16 [24576, 2, 1024], P('seq', None, 'head'), may hold values from -6 to 6
- gate_in: bfloat16 [24576, 8192], P('seq', 'head'), may hold values from -6 to 6
- step_size: float32 [24576, 128], P('seq', 'head'), may hold values from 0 to 1
- decay_rate: float32 [128], P('head'), may hold values from 0.5 to 2
- skip: float32 [128], P('head'), may hold values from 0.5 to 1.5
- conv_x: bfloat16 [4, 8192], P(None, 'head'), may hold values from -3 to 3
- conv_bc: bfloat16 [4, 2, 1024], P(None, None, 'head'), may hold values from -3 to 3
- norm_gain: float32 [8192], P('head'), may hold values from 0.1 to 1.9
- queries: bfloat16 [24576, 2048], P(('seq', 'head')), may hold values from -9 to 9
- keys_values: bfloat16 [24576, 2, 512], P(('seq', 'head')), may hold values from -9 to 9
- doc_lengths: int32 [16], replicated, may hold values from 1 to 3072, 24576 in all
Outputs:
- mamba_out: bfloat16 [24576, 8192], P('seq', 'head')
- attn_out: bfloat16 [24576, 2048], P('seq', 'head')
All inputs are finite; a program needn't handle non-finite values.
Results may differ from a plain program's by a relative error of at most 0.007.
Values may be sent and summed in bfloat16 or wider, within the bound.
A program may use at most 192 MiB of HBM per device.

v0:
```python
import functools
import jax
import jax.numpy as jnp
from jax import lax
from jax.experimental import pallas as pl
from jax.experimental.pallas import tpu as pltpu
from jax.sharding import PartitionSpec as P

T = 384
CH = 64
NC = T // CH
HD = 64
ST = 128
NH = 32
GC = 1024
INNER = 2 * GC
AD = 128
QH = 4
DOCS = 16
HALO = 16
BLOCKS = 64
EPSILON = 1e-05
MASKED = -1e30
SCORE = 1.4426950408889634 / AD**0.5
MESH = pl.DeviceIdType.MESH
F32 = jnp.float32
BF16 = jnp.bfloat16

Z, XP, XM, RP, RM = range(5)


def mm(a, b):
    return jnp.dot(a, b, preferred_element_type=F32)


def mm_nt(a, b):
    return lax.dot_general(a, b, (((1,), (1,)), ((), ())), preferred_element_type=F32)


def silu(v):
    half = 0.5 * v
    return half + half * jnp.tanh(half)


def split_rows(v):
    lane = lax.broadcasted_iota(jnp.int32, v.shape, 1)
    v = jnp.where(lane < NH, v, 0.0)
    high = v.astype(BF16).astype(F32)
    return (high + pltpu.roll(v - high, NH, 1)).astype(BF16)


def kernel(
    dl_ref, dec_ref, skip_ref, cx_ref, cbc_ref, gain_ref,
    x_ref, bc_ref, gate_ref, step_ref, q_ref, kv_ref,
    mo_ref, ao_ref,
    xb, bcb, gb, stt, qb, qa, kvb, cf, start, masks, xc, xs, bm, cc, ex, cum, cumd, hp, sdev, srecv, sb, tin,
    uhl, ehl, rows_sc, rex, yg, eg, ob, ab, sc, pb, mrow, lrow, arow, acc,
    loc_s, a_s, a_r, halo_s, halo_r, kv_s, kv_r, sh_s, st_s, st_r, sx_s, sx_r, tx_s, tx_r, out_s,
):
    s = lax.axis_index("seq")
    h = lax.axis_index("head")
    core = lax.rem(s, 2)
    x = lax.rem(s // 2, 4)
    z = s // 8
    first_row = s * T

    def at(zz, xx, cc_):
        return {"seq": (zz * 4 + xx) * 2 + cc_, "head": h}

    nz = lax.axis_size("seq") // 8
    z_next, z_prev = lax.rem(z + 1, nz), lax.rem(z + nz - 1, nz)
    x_next, x_prev = lax.rem(x + 1, 4), lax.rem(x + 3, 4)
    sibling = at(z, x, 1 - core)
    above, below = at(z_next, x, core), at(z_prev, x, core)
    right, left = at(z, x_next, core), at(z, x_prev, core)
    after = {"seq": lax.rem(s + 1, nz * 8), "head": h}
    before = {"seq": lax.rem(s + nz * 8 - 1, nz * 8), "head": h}

    def peer(o):
        return lax.rem(h + o, 4)

    def remote(src, dst, ssem, rsem, target):
        return pltpu.make_async_remote_copy(
            src_ref=src, dst_ref=dst, send_sem=ssem, recv_sem=rsem, device_id=target, device_id_type=MESH
        )

    loads = [
        pltpu.make_async_copy(x_ref, xb.at[pl.ds(HALO, T)], loc_s.at[0]),
        pltpu.make_async_copy(bc_ref, bcb.at[pl.ds(HALO, T)], loc_s.at[1]),
        pltpu.make_async_copy(step_ref, stt.at[pl.ds(0, NH)], loc_s.at[2]),
        pltpu.make_async_copy(gate_ref, gb, loc_s.at[3]),
        pltpu.make_async_copy(
            q_ref.at[:, pl.ds(pl.multiple_of(h * 512, 512), 512)],
            qb.at[pl.ds(pl.multiple_of(h * 96, 32), 96)], loc_s.at[4]),
        pltpu.make_async_copy(
            kv_ref.at[:, pl.ds(pl.multiple_of(h * 256, 256), 256)],
            kvb.at[0, pl.ds(pl.multiple_of(h * 96, 32), 96), pl.ds(0, 256)], loc_s.at[5]),
    ]
    for copy in loads:
        copy.start()

    barrier = pltpu.get_barrier_semaphore()
    for o in (1, 2, 3):
        pl.semaphore_signal(barrier, inc=1, device_id={"seq": s, "head": peer(o)}, device_id_type=MESH)
    for target in (before, sibling, below, left, right):
        pl.semaphore_signal(barrier, inc=1, device_id=target, device_id_type=MESH)
    pl.semaphore_wait(barrier, 8)

    def a2a(o, which):
        to = peer(o)
        target = {"seq": s, "head": to}
        mine = pl.ds(pl.multiple_of(h * 96, 32), 96)
        if which == 0:
            return remote(
                kv_ref.at[:, pl.ds(pl.multiple_of(to * 256, 256), 256)], kvb.at[0, mine, pl.ds(0, 256)],
                a_s.at[0, o - 1], a_r.at[0, o - 1], target)
        return remote(
            q_ref.at[:, pl.ds(pl.multiple_of(to * 512, 512), 512)], qb.at[mine],
            a_s.at[1, o - 1], a_r.at[1, o - 1], target)

    halo_x = remote(x_ref.at[pl.ds(T - HALO, HALO)], xb.at[pl.ds(0, HALO)], halo_s.at[0], halo_r.at[0], after)
    halo_bc = remote(bc_ref.at[pl.ds(T - HALO, HALO)], bcb.at[pl.ds(0, HALO)], halo_s.at[1], halo_r.at[1], after)
    halo_x.start()
    halo_bc.start()
    exchange = [[a2a(o, w) for o in (1, 2, 3)] for w in (0, 1)]
    for group in exchange:
        for copy in group:
            copy.start()

    def relay(buf, ssem, rsem, stride):
        def slot(d):
            return buf(d * stride)

        def copy(src, dst, k, target):
            return remote(slot(src), slot(dst), ssem.at[k], rsem.at[dst - 1], target)

        up = copy(0, 4, Z, above)
        right_own, right_far = copy(0, 1, XP, right), copy(4, 1, XP, right)
        left_own, left_far = copy(0, 3, XM, left), copy(4, 3, XM, left)
        hop_right, hop_left = copy(1, 2, RP, right), copy(3, 2, RM, left)
        inner = (x == 1) | (x == 2)

        def start_own():
            up.start()
            pl.when(x < 3)(right_own.start)
            pl.when(x == 0)(left_own.start)

        def arrived_4():
            up.wait_recv()
            pl.when(x == 3)(right_far.start)
            pl.when(x > 0)(left_far.start)

        def arrived_1():
            right_own.wait_recv()
            pl.when(inner)(hop_right.start)

        def arrived_3():
            left_own.wait_recv()
            pl.when(inner)(hop_left.start)

        def arrived_2():
            hop_right.wait_recv()

        def sent():
            up.wait_send()
            right_own.wait_send()
            left_own.wait_send()

            @pl.when(inner)
            def _():
                hop_right.wait_send()
                hop_left.wait_send()

        return start_own, arrived_4, arrived_1, arrived_3, arrived_2, sent

    kv_own, kv_4, kv_1, kv_3, kv_2, kv_sent = relay(lambda d: kvb.at[d, :, pl.ds(0, 256)], kv_s, kv_r, 2)
    st_own, st_4, st_1, st_3, st_2, st_sent = relay(lambda d: sb.at[d], st_s, st_r, 1)

    def share(i):
        return remote(
            kvb.at[2 * (i + core), :, pl.ds(0, 256)], kvb.at[2 * i + 1, :, pl.ds(0, 256)],
            sh_s.at[i], kv_r.at[4 + i], sibling)

    def share_slot(d):
        if d == 0:
            pl.when(core == 0)(share(0).start)
        elif d == 8:
            pl.when(core == 1)(share(3).start)
        else:
            for c in (0, 1):
                pl.when(core == c)(share(d // 2 - c).start)

    ends, total = [], jnp.int32(0)
    for i in range(DOCS):
        total = total + dl_ref[i]
        ends.append(total)
    row = lax.broadcasted_iota(jnp.int32, (T, 128), 0)
    lane = lax.broadcasted_iota(jnp.int32, (T, 128), 1)
    pos = row + first_row
    begin = jnp.zeros((T, 128), jnp.int32)
    for i in range(DOCS):
        begin = jnp.where(ends[i] <= pos, ends[i], begin)
    start[...] = begin
    inside = pos - begin
    for lag in (1, 2, 3):
        masks[lag - 1] = jnp.where(inside >= lag, 1.0, 0.0)
    lane1 = lax.broadcasted_iota(jnp.int32, (1, 128), 1)
    doc_first = jnp.full((1, 128), 1 << 30, jnp.int32)
    doc_end = jnp.full((1, 128), 1 << 30, jnp.int32)
    for i in range(DOCS):
        doc_end = jnp.where(lane1 == i, ends[i], doc_end)
        doc_first = jnp.where(lane1 == i, ends[i - 1] if i else 0, doc_first)
    for d in range(9):
        block = lax.rem(s + BLOCKS - d, BLOCKS)
        key = row + block * T
        hot = (key >= doc_first) & (key < doc_end)
        kvb[d, :, pl.ds(256, 128)] = jnp.where(hot, 1.0, 0.0).astype(BF16)
        if d == 0:
            blind = jnp.where(hot | (lane >= DOCS), 0.0, MASKED).astype(BF16)
            for i in range(QH):
                qa[i, :, pl.ds(128, 128)] = blind

    def expand_body(n, carry):
        r = lax.broadcasted_iota(jnp.int32, (128, 256), 0)
        c = lax.broadcasted_iota(jnp.int32, (128, 256), 1) + n * 256
        ex[:, pl.ds(pl.multiple_of(n * 256, 256), 256)] = jnp.where(
            (r < 2 * NH) & (lax.rem(r, NH) == c // HD), 1.0, 0.0).astype(BF16)
        return carry

    lax.fori_loop(0, INNER // 256, expand_body, 0)

    rows_sc[...] = jnp.zeros_like(rows_sc)
    rows_sc[pl.ds(32, 1), pl.ds(0, NH)] = dec_ref[...].reshape(1, NH)
    rows_sc[pl.ds(25, 1), pl.ds(0, NH)] = skip_ref[...].reshape(1, NH)
    loads[2].wait()
    stt[pl.ds(NH, 128 - NH)] = jnp.zeros((128 - NH, T), F32)
    step = jnp.transpose(stt[...])
    a = -(step * rows_sc[pl.ds(32, 1), :])
    a1 = a.astype(BF16).astype(F32)
    a2 = (a - a1).astype(BF16).astype(F32)
    a3 = a - a1 - a2
    parts = (a1 + pltpu.roll(a2, 32, 1) + pltpu.roll(a3, 64, 1)).astype(BF16)
    tr = lax.broadcasted_iota(jnp.int32, (T, T), 0)
    tc = lax.broadcasted_iota(jnp.int32, (T, T), 1)
    tri = jnp.where(tc <= tr, 1.0, 0.0)
    tri_ch = jnp.where((tc <= tr) & (tc // CH == tr // CH), 1.0, 0.0)

    def collect(t):
        v = mm(t.astype(BF16), parts)
        v = v + pltpu.roll(v, 96, 1) + pltpu.roll(v, 64, 1)
        return jnp.where(lane < NH, v, 0.0)

    cum[...] = collect(tri_ch)
    cumd[...] = collect(tri)
    for c in range(NC):
        rc = pl.ds(c * CH, CH)
        cu = cum[rc, :]
        mid = cum[pl.ds(c * CH + CH // 2 - 1, 1), :]
        end = cum[pl.ds(c * CH + CH - 1, 1), :]
        uhl[rc, :] = split_rows(jnp.exp(cu - mid))
        through = jnp.where(start[pl.ds(c * CH + CH - 1, 1), :] < first_row + c * CH, 1.0, 0.0)
        rows_sc[pl.ds(c, 1), :] = jnp.exp(mid)
        rows_sc[pl.ds(8 + c, 1), :] = jnp.exp(end - mid)
        rows_sc[pl.ds(16 + c, 1), :] = jnp.exp(end) * through
        cum[rc, :] = step[c * CH : (c + 1) * CH] * jnp.exp(mid - cu)
    open_dev = jnp.where(start[pl.ds(T - 1, 1), :] < first_row, 1.0, 0.0)
    rows_sc[pl.ds(24, 1), :] = jnp.exp(cumd[pl.ds(T - 1, 1), :]) * open_dev
    ehl[...] = split_rows(jnp.where(start[...] < first_row, jnp.exp(cumd[...]), 0.0))
    rex[...] = mm(split_rows(rows_sc[pl.ds(0, 32), :]), ex[...])
    svhl = split_rows(cum[...])

    loads[0].wait()
    loads[1].wait()
    halo_x.wait_recv()
    halo_bc.wait_recv()

    def convolve(src, cols, weight):
        cf[...] = src[:, cols].astype(F32)
        out = cf[pl.ds(HALO, T), :] * weight[3:4]
        for lag in (1, 2, 3):
            out = out + cf[pl.ds(HALO - lag, T), :] * masks[lag - 1] * weight[3 - lag : 4 - lag]
        return silu(out).astype(BF16)

    def conv_bc(n, carry):
        cols = pl.ds(pl.multiple_of(n * 128, 128), 128)
        out = convolve(bcb, cols, cbc_ref[:, cols].astype(F32))

        @pl.when(n < 2)
        def _():
            bm[:, cols] = out

        @pl.when(n >= 2)
        def _():
            cc[:, pl.ds(pl.multiple_of(n * 128 - 256, 128), 128)] = out
        return carry

    lax.fori_loop(0, 4, conv_bc, 0)

    def conv_x(n, carry):
        cols = pl.ds(pl.multiple_of(n * 128, 128), 128)
        out = convolve(xb, cols, cx_ref[:, cols].astype(F32))
        xc[:, cols] = out
        xs[:, cols] = (out.astype(F32) * mm(svhl, ex[:, cols])).astype(BF16)
        return carry

    lax.fori_loop(0, 16, conv_x, 0)

    loads[5].wait()
    for copy in exchange[0]:
        copy.wait_recv()
    kv_own()
    share_slot(0)

    def states(n, carry):
        cols = pl.ds(pl.multiple_of(n * 256, 256), 256)
        g = n // 4
        gl = pl.ds(pl.multiple_of(g * 128, 128), 128)
        gcols = pl.ds(pl.multiple_of(lax.rem(n, 4) * 256, 256), 256)
        state = jnp.zeros((ST, 256), F32)
        for c in range(NC):
            rc = pl.ds(c * CH, CH)
            hp[c, :, cols] = (state * rex[pl.ds(c, 1), cols]).astype(BF16)
            last = start[pl.ds(c * CH + CH - 1, 1), :]
            b = jnp.where(pos[c * CH : (c + 1) * CH] >= last, bm[rc, gl].astype(F32), 0.0).astype(BF16)
            new = lax.dot_general(b, xs[rc, cols], (((0,), (0,)), ((), ())), preferred_element_type=F32)
            state = state * rex[pl.ds(16 + c, 1), cols] + new * rex[pl.ds(8 + c, 1), cols]
        sdev[g, pl.ds(0, ST), gcols] = state.astype(BF16)
        d = jnp.broadcast_to(rex[pl.ds(24, 1), cols], (8, 256))
        high = d.astype(BF16).astype(F32)
        sdev[g, pl.ds(ST, 16), gcols] = jnp.concatenate([high, d - high], 0).astype(BF16)
        return carry

    lax.fori_loop(0, 8, states, 0)
    swap = remote(sdev.at[1 - core], srecv, sx_s, sx_r, sibling)
    swap.start()

    def decay_of(ref, cols):
        d = ref[pl.ds(ST, 16), cols].astype(F32)
        return d[0:1] + d[8:9]

    def both(cols):
        mine, other = sdev.at[core], srecv
        sm, so = mine[pl.ds(0, ST), cols].astype(F32), other[pl.ds(0, ST), cols].astype(F32)
        dm, do = decay_of(mine, cols), decay_of(other, cols)
        first = core == 0
        return (jnp.where(first, sm, so), jnp.where(first, dm, do), jnp.where(first, so, sm), jnp.where(first, do, dm))

    loads[4].wait()
    for copy in exchange[1]:
        copy.wait_recv()
    for i in range(QH):
        qa[i, :, pl.ds(0, 128)] = qb[:, pl.ds(i * 128, 128)]

    swap.wait_recv()

    def chip_state(n, carry):
        cols = pl.ds(pl.multiple_of(n * 256, 256), 256)
        s0, d0, s1, d1 = both(cols)
        sb[0, pl.ds(0, ST), cols] = (s0 * d1 + s1).astype(BF16)
        d = jnp.broadcast_to(d0 * d1, (8, 256))
        high = d.astype(BF16).astype(F32)
        sb[0, pl.ds(ST, 16), cols] = jnp.concatenate([high, d - high], 0).astype(BF16)
        return carry

    lax.fori_loop(0, 4, chip_state, 0)
    st_own()

    RT = 64

    def attend(slots, first):
        width = T * len(slots)

        def head(i, carry):
            for n, d in enumerate(slots):
                sc[:, pl.ds(n * T, T)] = mm_nt(qa[i], kvb[d, :, pl.ds(128, 256)])

            def tile(r, carry):
                rs = pl.ds(pl.multiple_of(r * RT, RT), RT)
                v = sc[rs, pl.ds(0, width)]
                if first:
                    rr = lax.broadcasted_iota(jnp.int32, (RT, T), 0) + r * RT
                    rc = lax.broadcasted_iota(jnp.int32, (RT, T), 1)
                    own = jnp.where(rc <= rr, v[:, :T], MASKED)
                    v = own if width == T else jnp.concatenate([own, v[:, T:]], 1)
                top = jnp.max(v, axis=1, keepdims=True)
                if not first:
                    old = mrow[i, rs, :]
                    new = jnp.maximum(old, top)
                    fade = jnp.exp2((old - new) * SCORE)
                    arow[rs, :] = fade
                    top = new[:, 0:1]
                else:
                    new = jnp.broadcast_to(top, (RT, 128))
                mrow[i, rs, :] = new
                p = jnp.exp2((v - top) * SCORE)
                part = p[:, 0:128]
                for k in range(1, width // 128):
                    part = part + p[:, k * 128 : (k + 1) * 128]
                lrow[i, rs, :] = part if first else lrow[i, rs, :] * fade + part
                pb[rs, pl.ds(0, width)] = p.astype(BF16)
                return carry

            lax.fori_loop(0, T // RT, tile, 0)
            out = mm(pb[:, pl.ds(0, T)], kvb[slots[0], :, pl.ds(0, 128)])
            for n, d in enumerate(slots[1:]):
                out = out + mm(pb[:, pl.ds((n + 1) * T, T)], kvb[d, :, pl.ds(0, 128)])
            acc[i] = out if first else acc[i] * arow[...] + out
            return carry

        lax.fori_loop(0, QH, head, 0)

    attend((0,), True)

    loads[3].wait()

    def local(k, carry):
        c, g = k // 2, lax.rem(k, 2)
        rc = pl.ds(pl.multiple_of(c * CH, CH), CH)
        gl = pl.ds(pl.multiple_of(g * 128, 128), 128)
        begin = start[rc, :]
        base = first_row + c * CH
        tpos = lax.broadcasted_iota(jnp.int32, (CH, CH), 0)
        spos = lax.broadcasted_iota(jnp.int32, (CH, CH), 1)
        cg = cc[rc, gl]
        grid = mm_nt(cg, bm[rc, gl])
        grid = jnp.where((spos <= tpos) & (spos + base >= begin[:, :CH]), grid, 0.0).astype(BF16)
        open_c = jnp.where(begin < base, cg.astype(F32), 0.0).astype(BF16)
        u, e = uhl[rc, :], ehl[rc, :]
        for n in range(4):
            cols = pl.ds(pl.multiple_of(g * GC + n * 256, 256), 256)
            y = mm(grid, xs[rc, cols]) + mm(open_c, hp[c, :, cols])
            y = y * mm(u, ex[:, cols]) + rex[pl.ds(25, 1), cols] * xc[rc, cols].astype(F32)
            sg = silu(gb[rc, cols].astype(F32))
            yg[rc, cols] = y * sg
            eg[rc, cols] = mm(e, ex[:, cols]) * sg
        return carry

    def locals_(lo, hi):
        lax.fori_loop(lo, hi, local, 0)

    locals_(0, 4)
    kv_4()
    share_slot(8)
    kv_1()
    share_slot(2)
    kv_3()
    share_slot(6)
    locals_(4, 8)
    st_4()
    locals_(8, 12)

    def kv_odd(i):
        share(i).wait_recv()

    kv_odd(0)
    attend((1, 2, 8), False)
    kv_2()
    share_slot(4)
    st_1()
    st_3()
    kv_odd(1)
    kv_odd(3)
    attend((3, 6, 7), False)
    kv_odd(2)
    attend((4, 5), False)

    def finish_head(i, carry):
        total = jnp.sum(lrow[i], axis=1, keepdims=True)
        ab[:, pl.ds(pl.multiple_of(i * 128, 128), 128)] = (acc[i] / total).astype(BF16)
        return carry

    lax.fori_loop(0, QH, finish_head, 0)
    out_a = pltpu.make_async_copy(ab, ao_ref, out_s.at[0])
    out_a.start()

    st_2()

    def enter(n, carry):
        cols = pl.ds(pl.multiple_of(n * 256, 256), 256)
        t = sb[4, pl.ds(0, ST), cols].astype(F32)
        for d in (3, 2, 1):
            t = sb[d, pl.ds(0, ST), cols].astype(F32) + decay_of(sb.at[d], cols) * t
        s0, d0, _, _ = both(cols)
        t1 = s0 + d0 * t
        first = core == 0
        tin[core, :, cols] = jnp.where(first, t, t1).astype(BF16)
        srecv2[:, cols] = jnp.where(first, t1, t).astype(BF16)
        return carry

    srecv2 = hp.at[0, :, pl.ds(0, GC)]
    lax.fori_loop(0, 4, enter, 0)
    give = remote(srecv2, tin.at[core], tx_s, tx_r, sibling)
    give.start()
    remote(srecv2, tin.at[1 - core], tx_s, tx_r, sibling).wait_recv()

    def tail(k, carry):
        c, g = k // 2, lax.rem(k, 2)
        rc = pl.ds(pl.multiple_of(c * CH, CH), CH)
        gl = pl.ds(pl.multiple_of(g * 128, 128), 128)
        gcols = pl.ds(pl.multiple_of(g * GC, GC), GC)
        gated = yg[rc, gcols] + eg[rc, gcols] * mm(cc[rc, gl], tin[g])
        mean = jnp.sum(gated * gated, axis=1, keepdims=True) * (1.0 / GC)
        scale = lax.rsqrt(mean + EPSILON)
        ob[rc, gcols] = (gated * scale * gain_ref[gcols].reshape(1, GC)).astype(BF16)
        pltpu.make_async_copy(ob.at[rc, gcols], mo_ref.at[rc, gcols], out_s.at[1]).start()
        return carry

    lax.fori_loop(0, 2 * NC, tail, 0)

    for group in exchange:
        for copy in group:
            copy.wait_send()
    halo_x.wait_send()
    halo_bc.wait_send()
    kv_sent()
    st_sent()
    for i in range(4):
        share(i).wait_send()
    swap.wait_send()
    give.wait_send()
    out_a.wait()
    pltpu.make_async_copy(ob, mo_ref, out_s.at[1]).wait()


def per_device(
    x_in, bc_in, gate_in, step_size, decay_rate, skip, conv_x, conv_bc, norm_gain, queries, keys_values, doc_lengths
):
    bc = bc_in.reshape(T, 512)
    cbc = conv_bc.reshape(4, 512)
    kv = jnp.stack(
        [keys_values[:, 1].reshape(96, 4, AD), keys_values[:, 0].reshape(96, 4, AD)], axis=2
    ).reshape(96, 1024)
    vm, hbm = pl.BlockSpec(memory_space=pltpu.VMEM), pl.BlockSpec(memory_space=pl.ANY)
    dma = pltpu.SemaphoreType.DMA
    V = pltpu.VMEM
    return pl.pallas_call(
        kernel,
        out_shape=(jax.ShapeDtypeStruct((T, INNER), BF16), jax.ShapeDtypeStruct((T, QH * AD), BF16)),
        in_specs=[pl.BlockSpec(memory_space=pltpu.SMEM)] + [vm] * 5 + [hbm] * 6,
        out_specs=(hbm, hbm),
        scratch_shapes=[
            V((HALO + T, INNER), BF16),
            V((HALO + T, 512), BF16),
            V((T, INNER), BF16),
            V((128, T), F32),
            V((T, 512), BF16),
            V((QH, T, 256), BF16),
            V((9, T, 384), BF16),
            V((HALO + T, 128), F32),
            V((T, 128), jnp.int32),
            V((3, T, 128), F32),
            V((T, INNER), BF16),
            V((T, INNER), BF16),
            V((T, 256), BF16),
            V((T, 256), BF16),
            V((128, INNER), BF16),
            V((T, 128), F32),
            V((T, 128), F32),
            V((NC, ST, INNER), BF16),
            V((2, ST + 16, GC), BF16),
            V((ST + 16, GC), BF16),
            V((5, ST + 16, GC), BF16),
            V((2, ST, GC), BF16),
            V((T, 128), BF16),
            V((T, 128), BF16),
            V((40, 128), F32),
            V((32, INNER), F32),
            V((T, INNER), F32),
            V((T, INNER), F32),
            V((T, INNER), BF16),
            V((T, 512), BF16),
            V((T, 3 * T), F32),
            V((T, 3 * T), BF16),
            V((QH, T, 128), F32),
            V((QH, T, 128), F32),
            V((T, 128), F32),
            V((QH, T, 128), F32),
            dma((6,)),
            dma((2, 3)),
            dma((2, 3)),
            dma((2,)),
            dma((2,)),
            dma((5,)),
            dma((8,)),
            dma((4,)),
            dma((5,)),
            dma((4,)),
            dma,
            dma,
            dma,
            dma,
            dma((2,)),
        ],
        compiler_params=pltpu.CompilerParams(
            collective_id=0, has_side_effects=True, vmem_limit_bytes=60 * 1024 * 1024
        ),
        name="hybrid",
    )(doc_lengths, decay_rate, skip, conv_x, cbc, norm_gain, x_in, bc, gate_in, step_size.T, queries, kv)


def solution(mesh):
    placed = (
        P("seq", "head"),
        P("seq", None, "head"),
        P("seq", "head"),
        P("seq", "head"),
        P("head"),
        P("head"),
        P(None, "head"),
        P(None, None, "head"),
        P("head"),
        P(("seq", "head"), None),
        P(("seq", "head"), None, None),
        P(),
    )
    return jax.shard_map(
        per_device,
        mesh=mesh,
        in_specs=placed,
        out_specs=(P("seq", "head"), P("seq", "head")),
        check_vma=False,
    )
```

profile of v0, /device:TPU:1, one launch (start us, length us, event | category | flops | bytes accessed | tf_op | source)
XLA Modules:
  0.0 76.3 jit_solution(3068524176380513374)
XLA Ops:
  0.6 0.0 copy-start
  0.6 1.3 %copy.17 = bf16[1,4,2,256]{3,1,2,0:T(4,128)(2,1)} copy(bf16[1,4,2,256]{3,2,1,0:T(2,128)(2,1)} %bitcast.9) | data formatting | bytes 8192
  2.0 1.9 %slice_reduce_fusion.1 = (bf16[96,512]{1,0:T(8,128)(2,1)S(1)}, bf16[96,512]{1,0:T(8,128)(2,1)S(1)}) fusion(bf16[96,2,512]{2,1,0:T(2,128)(2,1)} %param.22), kind=kLoop, calls=%fused_computation.2 | loop fusion | bytes 393216 | tf_op jit(solution)/shard_map/slice | solution.py:531
  3.9 0.1 pad_maximum_fusion
  4.1 0.3 copy.16
  4.3 0.8 %reshape.15.kv_ref = bf16[96,1024]{1,0:T(8,128)(2,1)} reshape(bf16[96,4,2,128]{3,2,1,0:T(2,128)(2,1)S(1)} %copy.16) | data formatting | bytes 393216 | tf_op jit(solution)/shard_map/reshape | solution.py:532
  5.1 0.0 copy-done
  5.1 0.8 %copy.18 = bf16[48,8,2,256]{3,1,2,0:T(8,128)(2,1)} copy(bf16[48,8,2,256]{3,2,1,0:T(2,128)(2,1)S(1)} %bitcast.6) | data formatting | bytes 786432
  5.9 66.8 %hybrid.1 = (bf16[384,2048]{1,0:T(8,128)(2,1)}, bf16[384,512]{1,0:T(8,128)(2,1)}) custom-call(s32[16]{0:T(128)} %dl_ref.1, f32[32]{0:T(128)} %dec_ref.1, f32[32]{0:T(128)} %skip_ref.1, bf16[4,2048]{1,0:T(4,128)(2,1)} %cx_ref.1, bf16[4,512]{1,0:T(4,128)(2,1)} %bitcast.8, f32[2048]{0:T(1024)} %gain_ref.1, bf16[384,2048]{1,0:T(8,128)(2,1)} %x_ref.1, ...), custom_call_target="tpu_custom_call" | custom-call | tf_op jit(solution)/shard_map/hybrid/pallas_call | solution.py:536
  72.8 0.0 copy-start.1
  72.8 2.8 %copy.21 = bf16[384,2048]{1,0:T(8,128)(2,1)} copy(bf16[384,2048]{1,0:T(8,128)(2,1)} %get-tuple-element.6) | data formatting | bytes 3145728
  75.6 0.0 copy-done.1
  75.6 0.7 copy.22
  (2 shorter events, 0.1 us)
Async XLA Ops:
  0.6 4.5 %copy-start = (bf16[384,2,256]{2,1,0:T(2,128)(2,1)S(1)}, bf16[384,2,256]{2,1,0:T(2,128)(2,1)}, u32[]{:S(2)}) copy-start(bf16[384,2,256]{2,1,0:T(2,128)(2,1)} %param.13) | copy-start | bytes 1179652
  72.8 2.8 %copy-start.1 = (bf16[384,512]{1,0:T(8,128)(2,1)S(1)}, bf16[384,512]{1,0:T(8,128)(2,1)}, u32[]{:S(2)}) copy-start(bf16[384,512]{1,0:T(8,128)(2,1)} %get-tuple-element.7) | copy-start | bytes 1179652
where the time goes:
time: 76.5 us; the launch traced here: 76.3 us
  Pallas kernels  66.8 us (87%)
  local copies, waits for them, and re-layouts  8.67 us (11%)
    pallas_call x1, Pallas kernels, per_device(): pl.pallas_call(kernel, out_shape=(jax.ShapeDtypeStruct((T, INNER), BF16),...  66.8 us
    unnamed x8, local copies, waits for them, and re-layouts  5.66 us
    slice x1, local copies, waits for them, and re-layouts, per_device(): keys_values[:, 1].reshape(96, 4, AD)  1.88 us

commit v1 on v0

--- a/solution.py
+++ b/solution.py
@@ -50,11 +50,11 @@
 
 
 def kernel(
-    dl_ref, dec_ref, skip_ref, cx_ref, cbc_ref, gain_ref,
+    dl_ref, dec_ref, skip_ref, cx_ref, cbc_ref,
     x_ref, bc_ref, gate_ref, step_ref, q_ref, kv_ref,
-    mo_ref, ao_ref,
-    xb, bcb, gb, stt, qb, qa, kvb, cf, start, masks, xc, xs, bm, cc, ex, cum, cumd, hp, sdev, srecv, sb, tin,
-    uhl, ehl, rows_sc, rex, yg, eg, ob, ab, sc, pb, mrow, lrow, arow, acc,
+    yg_ref, eg_ref, cc_ref, tin_ref, ao_ref,
+    xb, bc3, bcb, cbc, gb, stt, qb, qa, kv3, kvb, cf, start, masks, xc, xs, bm, cc, ex, cum, cumd, hp, sdev, srecv, sb, tin,
+    uhl, ehl, rows_sc, rex, yg, eg, ab, sc0, sc1, pb0, pb1, mrow, lrow, ar0, ar1, acc,
     loc_s, a_s, a_r, halo_s, halo_r, kv_s, kv_r, sh_s, st_s, st_r, sx_s, sx_r, tx_s, tx_r, out_s,
 ):
     s = lax.axis_index("seq")
@@ -86,15 +86,15 @@
 
     loads = [
         pltpu.make_async_copy(x_ref, xb.at[pl.ds(HALO, T)], loc_s.at[0]),
-        pltpu.make_async_copy(bc_ref, bcb.at[pl.ds(HALO, T)], loc_s.at[1]),
+        pltpu.make_async_copy(bc_ref, bc3.at[pl.ds(HALO, T)], loc_s.at[1]),
         pltpu.make_async_copy(step_ref, stt.at[pl.ds(0, NH)], loc_s.at[2]),
         pltpu.make_async_copy(gate_ref, gb, loc_s.at[3]),
         pltpu.make_async_copy(
             q_ref.at[:, pl.ds(pl.multiple_of(h * 512, 512), 512)],
             qb.at[pl.ds(pl.multiple_of(h * 96, 32), 96)], loc_s.at[4]),
         pltpu.make_async_copy(
-            kv_ref.at[:, pl.ds(pl.multiple_of(h * 256, 256), 256)],
-            kvb.at[0, pl.ds(pl.multiple_of(h * 96, 32), 96), pl.ds(0, 256)], loc_s.at[5]),
+            kv_ref.at[:, :, pl.ds(pl.multiple_of(h * 128, 128), 128)],
+            kv3.at[pl.ds(pl.multiple_of(h * 96, 32), 96)], loc_s.at[5]),
     ]
     for copy in loads:
         copy.start()
@@ -112,20 +112,19 @@
         mine = pl.ds(pl.multiple_of(h * 96, 32), 96)
         if which == 0:
             return remote(
-                kv_ref.at[:, pl.ds(pl.multiple_of(to * 256, 256), 256)], kvb.at[0, mine, pl.ds(0, 256)],
+                kv_ref.at[:, :, pl.ds(pl.multiple_of(to * 128, 128), 128)], kv3.at[mine],
                 a_s.at[0, o - 1], a_r.at[0, o - 1], target)
         return remote(
             q_ref.at[:, pl.ds(pl.multiple_of(to * 512, 512), 512)], qb.at[mine],
             a_s.at[1, o - 1], a_r.at[1, o - 1], target)
 
     halo_x = remote(x_ref.at[pl.ds(T - HALO, HALO)], xb.at[pl.ds(0, HALO)], halo_s.at[0], halo_r.at[0], after)
-    halo_bc = remote(bc_ref.at[pl.ds(T - HALO, HALO)], bcb.at[pl.ds(0, HALO)], halo_s.at[1], halo_r.at[1], after)
+    halo_bc = remote(bc_ref.at[pl.ds(T - HALO, HALO)], bc3.at[pl.ds(0, HALO)], halo_s.at[1], halo_r.at[1], after)
     halo_x.start()
     halo_bc.start()
     exchange = [[a2a(o, w) for o in (1, 2, 3)] for w in (0, 1)]
-    for group in exchange:
-        for copy in group:
-            copy.start()
+    for copy in exchange[0]:
+        copy.start()
 
     def relay(buf, ssem, rsem, stride):
         def slot(d):
@@ -274,6 +273,13 @@
     halo_x.wait_recv()
     halo_bc.wait_recv()
 
+    split = jnp.swapaxes(bc3[...], 0, 1)
+    bcb[:, pl.ds(0, 256)] = split[0]
+    bcb[:, pl.ds(256, 256)] = split[1]
+    taps_bc = jnp.swapaxes(cbc_ref[...], 0, 1).astype(F32)
+    cbc[:, pl.ds(0, 256)] = taps_bc[0]
+    cbc[:, pl.ds(256, 256)] = taps_bc[1]
+
     def convolve(src, cols, weight):
         cf[...] = src[:, cols].astype(F32)
         out = cf[pl.ds(HALO, T), :] * weight[3:4]
@@ -283,7 +289,7 @@
 
     def conv_bc(n, carry):
         cols = pl.ds(pl.multiple_of(n * 128, 128), 128)
-        out = convolve(bcb, cols, cbc_ref[:, cols].astype(F32))
+        out = convolve(bcb, cols, cbc[:, cols])
 
         @pl.when(n < 2)
         def _():
@@ -295,6 +301,8 @@
         return carry
 
     lax.fori_loop(0, 4, conv_bc, 0)
+    out_c = pltpu.make_async_copy(cc, cc_ref, out_s.at[3])
+    out_c.start()
 
     def conv_x(n, carry):
         cols = pl.ds(pl.multiple_of(n * 128, 128), 128)
@@ -303,13 +311,19 @@
         xs[:, cols] = (out.astype(F32) * mm(svhl, ex[:, cols])).astype(BF16)
         return carry
 
-    lax.fori_loop(0, 16, conv_x, 0)
+    lax.fori_loop(0, 8, conv_x, 0)
 
     loads[5].wait()
     for copy in exchange[0]:
         copy.wait_recv()
+    pair = jnp.swapaxes(kv3[...], 0, 1)
+    kvb[0, :, pl.ds(0, 128)] = pair[1]
+    kvb[0, :, pl.ds(128, 128)] = pair[0]
     kv_own()
     share_slot(0)
+    for copy in exchange[1]:
+        copy.start()
+    lax.fori_loop(8, 16, conv_x, 0)
 
     def states(n, carry):
         cols = pl.ds(pl.multiple_of(n * 256, 256), 256)
@@ -365,49 +379,67 @@
     lax.fori_loop(0, 4, chip_state, 0)
     st_own()
 
-    RT = 64
+    RT = 128
+    scs, pbs, ars = (sc0, sc1), (pb0, pb1), (ar0, ar1)
 
     def attend(slots, first):
-        width = T * len(slots)
-
-        def head(i, carry):
+        tiles = T * len(slots) // 128
+
+        def scores(i):
             for n, d in enumerate(slots):
-                sc[:, pl.ds(n * T, T)] = mm_nt(qa[i], kvb[d, :, pl.ds(128, 256)])
-
-            def tile(r, carry):
-                rs = pl.ds(pl.multiple_of(r * RT, RT), RT)
-                v = sc[rs, pl.ds(0, width)]
-                if first:
-                    rr = lax.broadcasted_iota(jnp.int32, (RT, T), 0) + r * RT
-                    rc = lax.broadcasted_iota(jnp.int32, (RT, T), 1)
-                    own = jnp.where(rc <= rr, v[:, :T], MASKED)
-                    v = own if width == T else jnp.concatenate([own, v[:, T:]], 1)
-                top = jnp.max(v, axis=1, keepdims=True)
-                if not first:
-                    old = mrow[i, rs, :]
-                    new = jnp.maximum(old, top)
-                    fade = jnp.exp2((old - new) * SCORE)
-                    arow[rs, :] = fade
-                    top = new[:, 0:1]
-                else:
-                    new = jnp.broadcast_to(top, (RT, 128))
+                scs[i % 2][:, pl.ds(n * T, T)] = mm_nt(qa[i], kvb[d, :, pl.ds(128, 256)])
+
+        def block(i, r, k):
+            v = scs[i % 2][pl.ds(r * RT, RT), pl.ds(k * 128, 128)]
+            if first and k == r:
+                rr = lax.broadcasted_iota(jnp.int32, (RT, 128), 0)
+                cc_ = lax.broadcasted_iota(jnp.int32, (RT, 128), 1)
+                v = jnp.where(cc_ <= rr, v, MASKED)
+            return v
+
+        def highest(i, r):
+            rs = pl.ds(r * RT, RT)
+            top = block(i, r, 0)
+            for k in range(1, r + 1 if first else tiles):
+                top = jnp.maximum(top, block(i, r, k))
+            top = jnp.max(top, axis=1, keepdims=True)
+            if first:
+                mrow[i, rs, :] = jnp.broadcast_to(top, (RT, 128))
+            else:
+                old = mrow[i, rs, :]
+                new = jnp.maximum(old, top)
+                ars[i % 2][rs, :] = jnp.exp2((old - new) * SCORE)
                 mrow[i, rs, :] = new
-                p = jnp.exp2((v - top) * SCORE)
-                part = p[:, 0:128]
-                for k in range(1, width // 128):
-                    part = part + p[:, k * 128 : (k + 1) * 128]
-                lrow[i, rs, :] = part if first else lrow[i, rs, :] * fade + part
-                pb[rs, pl.ds(0, width)] = p.astype(BF16)
-                return carry
-
-            lax.fori_loop(0, T // RT, tile, 0)
-            out = mm(pb[:, pl.ds(0, T)], kvb[slots[0], :, pl.ds(0, 128)])
+
+        def weigh(i, r):
+            rs = pl.ds(r * RT, RT)
+            new, part = mrow[i, rs, :], None
+            for k in range(tiles):
+                if first and k > r:
+                    pbs[i % 2][rs, pl.ds(k * 128, 128)] = jnp.zeros((RT, 128), BF16)
+                    continue
+                p = jnp.exp2((block(i, r, k) - new) * SCORE)
+                part = p if part is None else part + p
+                pbs[i % 2][rs, pl.ds(k * 128, 128)] = p.astype(BF16)
+            lrow[i, rs, :] = part if first else lrow[i, rs, :] * ars[i % 2][rs, :] + part
+
+        def gather(i):
+            out = mm(pbs[i % 2][:, pl.ds(0, T)], kvb[slots[0], :, pl.ds(0, 128)])
             for n, d in enumerate(slots[1:]):
-                out = out + mm(pb[:, pl.ds((n + 1) * T, T)], kvb[d, :, pl.ds(0, 128)])
-            acc[i] = out if first else acc[i] * arow[...] + out
-            return carry
-
-        lax.fori_loop(0, QH, head, 0)
+                out = out + mm(pbs[i % 2][:, pl.ds((n + 1) * T, T)], kvb[d, :, pl.ds(0, 128)])
+            acc[i] = out if first else acc[i] * ars[i % 2][...] + out
+
+        scores(0)
+        for i in range(QH):
+            if i + 1 < QH:
+                scores(i + 1)
+            if i > 0:
+                gather(i - 1)
+            for r in range(T // RT):
+                highest(i, r)
+            for r in range(T // RT):
+                weigh(i, r)
+        gather(QH - 1)
 
     attend((0,), True)
 
@@ -431,8 +463,11 @@
             y = mm(grid, xs[rc, cols]) + mm(open_c, hp[c, :, cols])
             y = y * mm(u, ex[:, cols]) + rex[pl.ds(25, 1), cols] * xc[rc, cols].astype(F32)
             sg = silu(gb[rc, cols].astype(F32))
-            yg[rc, cols] = y * sg
-            eg[rc, cols] = mm(e, ex[:, cols]) * sg
+            yg[rc, cols] = (y * sg).astype(BF16)
+            eg[rc, cols] = (mm(e, ex[:, cols]) * sg).astype(BF16)
+        gcols = pl.ds(pl.multiple_of(g * GC, GC), GC)
+        pltpu.make_async_copy(yg.at[rc, gcols], yg_ref.at[rc, gcols], out_s.at[1]).start()
+        pltpu.make_async_copy(eg.at[rc, gcols], eg_ref.at[rc, gcols], out_s.at[2]).start()
         return carry
 
     def locals_(lo, hi):
@@ -493,20 +528,8 @@
     give.start()
     remote(srecv2, tin.at[1 - core], tx_s, tx_r, sibling).wait_recv()
 
-    def tail(k, carry):
-        c, g = k // 2, lax.rem(k, 2)
-        rc = pl.ds(pl.multiple_of(c * CH, CH), CH)
-        gl = pl.ds(pl.multiple_of(g * 128, 128), 128)
-        gcols = pl.ds(pl.multiple_of(g * GC, GC), GC)
-        gated = yg[rc, gcols] + eg[rc, gcols] * mm(cc[rc, gl], tin[g])
-        mean = jnp.sum(gated * gated, axis=1, keepdims=True) * (1.0 / GC)
-        scale = lax.rsqrt(mean + EPSILON)
-        ob[rc, gcols] = (gated * scale * gain_ref[gcols].reshape(1, GC)).astype(BF16)
-        pltpu.make_async_copy(ob.at[rc, gcols], mo_ref.at[rc, gcols], out_s.at[1]).start()
-        return carry
-
-    lax.fori_loop(0, 2 * NC, tail, 0)
-
+    out_t = pltpu.make_async_copy(tin, tin_ref, out_s.at[4])
+    out_t.start()
     for group in exchange:
         for copy in group:
             copy.wait_send()
@@ -519,32 +542,78 @@
     swap.wait_send()
     give.wait_send()
     out_a.wait()
-    pltpu.make_async_copy(ob, mo_ref, out_s.at[1]).wait()
+    pltpu.make_async_copy(yg, yg_ref, out_s.at[1]).wait()
+    pltpu.make_async_copy(eg, eg_ref, out_s.at[2]).wait()
+    out_c.wait()
+    out_t.wait()
+
+
+TR = 64
+
+
+def finish(yg_ref, eg_ref, cc_ref, tin_ref, gain_ref, a_ref, mo_ref, ao_ref, yg, eg, cc, tin, ab, ob, in_s, row_s, out_s):
+    small = [
+        pltpu.make_async_copy(tin_ref, tin, in_s.at[0]),
+        pltpu.make_async_copy(cc_ref, cc, in_s.at[1]),
+    ]
+    rows = [pl.ds(i * TR, TR) for i in range(T // TR)]
+    large = [
+        (pltpu.make_async_copy(yg_ref.at[r], yg.at[r], row_s.at[0, i]),
+         pltpu.make_async_copy(eg_ref.at[r], eg.at[r], row_s.at[1, i])) for i, r in enumerate(rows)
+    ]
+    attention = pltpu.make_async_copy(a_ref, ab, in_s.at[2])
+    for copy in small:
+        copy.start()
+    for pair in large:
+        for copy in pair:
+            copy.start()
+    attention.start()
+    for copy in small:
+        copy.wait()
+    outs = []
+    for i, r in enumerate(rows):
+        for copy in large[i]:
+            copy.wait()
+        for g in range(2):
+            cols = pl.ds(g * GC, GC)
+            gated = yg[r, cols].astype(F32) + eg[r, cols].astype(F32) * mm(cc[r, pl.ds(g * 128, 128)], tin[g])
+            mean = jnp.sum(gated * gated, axis=1, keepdims=True) * (1.0 / GC)
+            scale = lax.rsqrt(mean + EPSILON)
+            ob[r, cols] = (gated * scale * gain_ref[cols].reshape(1, GC)).astype(BF16)
+        outs.append(pltpu.make_async_copy(ob.at[r], mo_ref.at[r], out_s.at[i]))
+        outs[-1].start()
+    attention.wait()
+    outs.append(pltpu.make_async_copy(ab, ao_ref, out_s.at[T // TR]))
+    outs[-1].start()
+    for copy in outs:
+        copy.wait()
 
 
 def per_device(
     x_in, bc_in, gate_in, step_size, decay_rate, skip, conv_x, conv_bc, norm_gain, queries, keys_values, doc_lengths
 ):
-    bc = bc_in.reshape(T, 512)
-    cbc = conv_bc.reshape(4, 512)
-    kv = jnp.stack(
-        [keys_values[:, 1].reshape(96, 4, AD), keys_values[:, 0].reshape(96, 4, AD)], axis=2
-    ).reshape(96, 1024)
     vm, hbm = pl.BlockSpec(memory_space=pltpu.VMEM), pl.BlockSpec(memory_space=pl.ANY)
     dma = pltpu.SemaphoreType.DMA
     V = pltpu.VMEM
-    return pl.pallas_call(
+    shape = jax.ShapeDtypeStruct
+    main = pl.pallas_call(
         kernel,
-        out_shape=(jax.ShapeDtypeStruct((T, INNER), BF16), jax.ShapeDtypeStruct((T, QH * AD), BF16)),
-        in_specs=[pl.BlockSpec(memory_space=pltpu.SMEM)] + [vm] * 5 + [hbm] * 6,
-        out_specs=(hbm, hbm),
+        out_shape=(
+            shape((T, INNER), BF16), shape((T, INNER), BF16), shape((T, 256), BF16),
+            shape((2, ST, GC), BF16), shape((T, QH * AD), BF16),
+        ),
+        in_specs=[pl.BlockSpec(memory_space=pltpu.SMEM)] + [vm] * 4 + [hbm] * 6,
+        out_specs=(hbm,) * 5,
         scratch_shapes=[
             V((HALO + T, INNER), BF16),
+            V((HALO + T, 2, 256), BF16),
             V((HALO + T, 512), BF16),
+            V((4, 512), F32),
             V((T, INNER), BF16),
             V((128, T), F32),
             V((T, 512), BF16),
             V((QH, T, 256), BF16),
+            V((T, 2, 128), BF16),
             V((9, T, 384), BF16),
             V((HALO + T, 128), F32),
             V((T, 128), jnp.int32),
@@ -565,14 +634,16 @@
             V((T, 128), BF16),
             V((40, 128), F32),
             V((32, INNER), F32),
-            V((T, INNER), F32),
-            V((T, INNER), F32),
+            V((T, INNER), BF16),
             V((T, INNER), BF16),
             V((T, 512), BF16),
             V((T, 3 * T), F32),
+            V((T, 3 * T), F32),
+            V((T, 3 * T), BF16),
             V((T, 3 * T), BF16),
             V((QH, T, 128), F32),
             V((QH, T, 128), F32),
+            V((T, 128), F32),
             V((T, 128), F32),
             V((QH, T, 128), F32),
             dma((6,)),
@@ -589,13 +660,28 @@
             dma,
             dma,
             dma,
-            dma((2,)),
+            dma((5,)),
         ],
         compiler_params=pltpu.CompilerParams(
             collective_id=0, has_side_effects=True, vmem_limit_bytes=60 * 1024 * 1024
         ),
         name="hybrid",
-    )(doc_lengths, decay_rate, skip, conv_x, cbc, norm_gain, x_in, bc, gate_in, step_size.T, queries, kv)
+    )
+    yg, eg, cc, tin, attended = main(
+        doc_lengths, decay_rate, skip, conv_x, conv_bc, x_in, bc_in, gate_in, step_size.T, queries, keys_values)
+    return pl.pallas_call(
+        finish,
+        out_shape=(shape((T, INNER), BF16), shape((T, QH * AD), BF16)),
+        in_specs=[hbm] * 4 + [vm, hbm],
+        out_specs=(hbm, hbm),
+        scratch_shapes=[
+            V((T, INNER), BF16), V((T, INNER), BF16), V((T, 256), BF16), V((2, ST, GC), BF16),
+            V((T, QH * AD), BF16), V((T, INNER), BF16),
+            dma((3,)), dma((2, T // TR)), dma((T // TR + 1,)),
+        ],
+        compiler_params=pltpu.CompilerParams(vmem_limit_bytes=60 * 1024 * 1024),
+        name="finish",
+    )(yg, eg, cc, tin, norm_gain, attended)
 
 
 def solution(mesh):

time: 76.5 us -> 56.4 us (0.74)
  the two profiles are of different devices: /device:TPU:1 before, /device:TPU:97 now
where the time goes in v1:
time: 56.4 us; the launch traced here: 56.2 us
  Pallas kernels  55.4 us (98%)
  between operations  0.8 us (1%)
    pallas_call x1, Pallas kernels, per_device(): main(doc_lengths, decay_rate, skip, conv_x, conv_bc, x_in, bc_in, gate_in...  49.8 us
    pallas_call x1, Pallas kernels, per_device(): pl.pallas_call(finish, out_shape=(shape((T, INNER), BF16), shape((T, QH *...  5.59 us

profile of v1, /device:TPU:97, one launch (start us, length us, event | category | flops | bytes accessed | tf_op | source)
XLA Modules:
  0.0 56.2 jit_solution(11028410242116950161)
XLA Ops:
  0.6 49.8 %hybrid.1 = (bf16[384,2048]{1,0:T(8,128)(2,1)}, bf16[384,2048]{1,0:T(8,128)(2,1)}, bf16[384,256]{1,0:T(8,128)(2,1)}, bf16[2,128,1024]{2,1,0:T(8,128)(2,1)}, bf16[384,512]{1,0:T(8,128)(2,1)}) custom-call(s32[16]{0:T(128)} %dl_ref.1, f32[32]{0:T(128)} %dec_ref.1, f32[32]{0:T(128)} %skip_ref.1, bf16[4,2048]{1,0:T(4,128)(2,1)} %cx_ref.1, ...), custom_call_target="tpu_custom_call" | custom-call | tf_op jit(solution)/shard_map/hybrid/pallas_call | solution.py:670
  50.4 5.6 %finish.1 = (bf16[384,2048]{1,0:T(8,128)(2,1)}, bf16[384,512]{1,0:T(8,128)(2,1)}) custom-call(bf16[384,2048]{1,0:T(8,128)(2,1)} %get-tuple-element.7.yg_ref, bf16[384,2048]{1,0:T(8,128)(2,1)} %get-tuple-element.8.eg_ref, bf16[384,256]{1,0:T(8,128)(2,1)} %get-tuple-element.9.cc_ref, bf16[2,128,1024]{2,1,0:T(8,128)(2,1)} %get-tuple-element.10.tin_ref, ...), custom_call_target="tpu_custom_call" | custom-call | tf_op jit(solution)/shard_map/finish/pallas_call | solution.py:672

commit v2 on v1

v2 whole, which is shorter than its diff:
```python
import functools
import jax
import jax.numpy as jnp
from jax import lax
from jax.experimental import pallas as pl
from jax.experimental.pallas import tpu as pltpu
from jax.sharding import PartitionSpec as P

T = 384
CH = 64
NC = T // CH
HD = 64
ST = 128
NH = 32
GC = 1024
INNER = 2 * GC
AD = 128
QH = 4
DOCS = 16
HALO = 16
BLOCKS = 64
EPSILON = 1e-05
MASKED = -1e30
SCORE = 1.4426950408889634 / AD**0.5
MESH = pl.DeviceIdType.MESH
F32 = jnp.float32
BF16 = jnp.bfloat16
HT = T // 2
NQ = GC // 4


def mm(a, b):
    return jnp.dot(a, b, preferred_element_type=F32)


def mm_nt(a, b):
    return lax.dot_general(a, b, (((1,), (1,)), ((), ())), preferred_element_type=F32)


def silu(v):
    half = 0.5 * v
    return half + half * jnp.tanh(half)


def split_rows(v):
    lane = lax.broadcasted_iota(jnp.int32, v.shape, 1)
    v = jnp.where(lane < NH, v, 0.0)
    high = v.astype(BF16).astype(F32)
    return (high + pltpu.roll(v - high, NH, 1)).astype(BF16)


def kernel(
    dl_ref, dec_ref, skip_ref, cx_ref, cbc_ref,
    x_ref, bc_ref, gate_ref, step_ref, q_ref, kv_ref,
    yg_ref, eg_ref, cc_ref, tin_ref, ao_ref,
    xb, hx, bc3, hb3, bcb, cbc, gb, stt, qb, qa, kv3, kvb, cf0, cf1, start, masks, xc, xh, fixed, fixed_s, bm, bt, mix, ex, cum, cumd, sdev, srecv, sq, got, tq, tback, give_b, tin,
    uhl, ehl, rows_sc, rex, ue, ee, yg, eg, cc, ab, sc0, sc1, pb0, pb1, mrow, lrow, ar0, ar1, acc,
    loc_s, a_s, a_r, halo_s, halo_r, z_s, z_r, row_s, row_r, sh_s, sh_r, st_s, st_r, tq_s, tq_r,
    sx_s, sx_r, tx_s, tx_r, out_s,
):
    s = lax.axis_index("seq")
    h = lax.axis_index("head")
    core = lax.rem(s, 2)
    x = lax.rem(s // 2, 4)
    z = s // 8
    first_row = s * T

    def at(zz, xx, cc_):
        return {"seq": (zz * 4 + xx) * 2 + cc_, "head": h}

    nz = lax.axis_size("seq") // 8
    z_next, z_prev = lax.rem(z + 1, nz), lax.rem(z + nz - 1, nz)
    right = [lax.rem(x + o, 4) for o in range(4)]
    left = [lax.rem(x + 4 - o, 4) for o in range(4)]
    sibling = at(z, x, 1 - core)
    above = at(z_next, x, core)
    after = {"seq": lax.rem(s + 1, nz * 8), "head": h}
    before = {"seq": lax.rem(s + nz * 8 - 1, nz * 8), "head": h}

    def peer(o):
        return lax.rem(h + o, 4)

    def remote(src, dst, ssem, rsem, target):
        return pltpu.make_async_remote_copy(
            src_ref=src, dst_ref=dst, send_sem=ssem, recv_sem=rsem, device_id=target, device_id_type=MESH
        )

    loads = [
        pltpu.make_async_copy(x_ref, xb.at[pl.ds(HALO, T)], loc_s.at[0]),
        pltpu.make_async_copy(bc_ref, bc3, loc_s.at[1]),
        pltpu.make_async_copy(step_ref, stt.at[pl.ds(0, NH)], loc_s.at[2]),
        pltpu.make_async_copy(gate_ref, gb, loc_s.at[3]),
        pltpu.make_async_copy(
            q_ref.at[:, pl.ds(pl.multiple_of(h * 512, 512), 512)],
            qb.at[pl.ds(pl.multiple_of(h * 96, 32), 96)], loc_s.at[4]),
        pltpu.make_async_copy(
            kv_ref.at[:, :, pl.ds(pl.multiple_of(h * 128, 128), 128)],
            kv3.at[pl.ds(pl.multiple_of(h * 96, 32), 96)], loc_s.at[5]),
    ]
    for copy in loads:
        copy.start()

    barrier = pltpu.get_barrier_semaphore()
    for o in (1, 2, 3):
        pl.semaphore_signal(barrier, inc=1, device_id={"seq": s, "head": peer(o)}, device_id_type=MESH)
    for target in (before, sibling):
        pl.semaphore_signal(barrier, inc=1, device_id=target, device_id_type=MESH)
    for o in (1, 2, 3):
        pl.semaphore_signal(barrier, inc=1, device_id=at(z, left[o], core), device_id_type=MESH)
    for o in (0, 1, 2, 3):
        pl.semaphore_signal(barrier, inc=1, device_id=at(z_prev, left[o], core), device_id_type=MESH)

    def a2a(o, which):
        to = peer(o)
        target = {"seq": s, "head": to}
        mine = pl.ds(pl.multiple_of(h * 96, 32), 96)
        if which == 0:
            return remote(
                kv_ref.at[:, :, pl.ds(pl.multiple_of(to * 128, 128), 128)], kv3.at[mine],
                a_s.at[0, o - 1], a_r.at[0, o - 1], target)
        return remote(
            q_ref.at[:, pl.ds(pl.multiple_of(to * 512, 512), 512)], qb.at[mine],
            a_s.at[1, o - 1], a_r.at[1, o - 1], target)

    halo_x = remote(x_ref.at[pl.ds(T - HALO, HALO)], hx, halo_s.at[0], halo_r.at[0], after)
    halo_bc = remote(bc_ref.at[pl.ds(T - HALO, HALO)], hb3, halo_s.at[1], halo_r.at[1], after)
    exchange = [[a2a(o, w) for o in (1, 2, 3)] for w in (0, 1)]

    def block_half(d, i):
        return kvb.at[d, pl.ds(i * HT, HT), pl.ds(0, 256)]

    rise = [remote(block_half(0, i), block_half(8, i), z_s.at[i], z_r.at[i], above) for i in (0, 1)]

    def along(o, i, source):
        return remote(
            block_half(source, i), block_half(2 * o, i), row_s.at[o - 1, i], row_r.at[o - 1, i], at(z, right[o], core))

    def kv_own():
        for copy in rise:
            copy.start()
        for o in (1, 2, 3):
            @pl.when(x + o < 4)
            def _():
                for i in (0, 1):
                    along(o, i, 0).start()

    def kv_risen(i):
        rise[i].wait_recv()
        for o in (3, 2, 1):
            pl.when(x + o >= 4)(along(o, i, 8).start)

    def kv_row(o):
        for i in (0, 1):
            along(o, i, 0).wait_recv()

    def share(i):
        return remote(
            kvb.at[2 * (i + core), :, pl.ds(0, 256)], kvb.at[2 * i + 1, :, pl.ds(0, 256)],
            sh_s.at[i], sh_r.at[i], sibling)

    def share_slot(d):
        if d == 0:
            pl.when(core == 0)(share(0).start)
        elif d == 8:
            pl.when(core == 1)(share(3).start)
        else:
            for c in (0, 1):
                pl.when(core == c)(share(d // 2 - c).start)

    def shared(d):
        if d in (0, 8):
            pl.when(core == 1)(share(0).wait_recv)
            pl.when(core == 0)(share(3).wait_recv)
        else:
            for c in (0, 1):
                pl.when(core == c)(share(d // 2 - 1 + c).wait_recv)

    ends, total = [], jnp.int32(0)
    for i in range(DOCS):
        total = total + dl_ref[i]
        ends.append(total)
    row = lax.broadcasted_iota(jnp.int32, (T, 128), 0)
    lane = lax.broadcasted_iota(jnp.int32, (T, 128), 1)
    pos = row + first_row
    begin = jnp.zeros((T, 128), jnp.int32)
    for i in range(DOCS):
        begin = jnp.where(ends[i] <= pos, ends[i], begin)
    start[...] = begin
    inside = pos - begin
    for lag in (1, 2, 3):
        masks[lag - 1] = jnp.where(inside >= lag, 1.0, 0.0)
    lane1 = lax.broadcasted_iota(jnp.int32, (1, 128), 1)
    doc_first = jnp.full((1, 128), 1 << 30, jnp.int32)
    doc_end = jnp.full((1, 128), 1 << 30, jnp.int32)
    for i in range(DOCS):
        doc_end = jnp.where(lane1 == i, ends[i], doc_end)
        doc_first = jnp.where(lane1 == i, ends[i - 1] if i else 0, doc_first)
    def expand_body(n, carry):
        r = lax.broadcasted_iota(jnp.int32, (128, 256), 0)
        c = lax.broadcasted_iota(jnp.int32, (128, 256), 1) + n * 256
        ex[:, pl.ds(pl.multiple_of(n * 256, 256), 256)] = jnp.where(
            (r < 2 * NH) & ((r & (NH - 1)) == (c >> 6)), 1.0, 0.0).astype(BF16)
        return carry

    lax.fori_loop(0, INNER // 256, expand_body, 0)

    rows_sc[...] = jnp.zeros_like(rows_sc)
    rows_sc[pl.ds(32, 1), pl.ds(0, NH)] = dec_ref[...].reshape(1, NH)
    rows_sc[pl.ds(25, 1), pl.ds(0, NH)] = skip_ref[...].reshape(1, NH)
    loads[2].wait()
    stt[pl.ds(NH, 128 - NH)] = jnp.zeros((128 - NH, T), F32)
    step = jnp.transpose(stt[...])
    a = -(step * rows_sc[pl.ds(32, 1), :])
    a1 = a.astype(BF16).astype(F32)
    a2 = (a - a1).astype(BF16).astype(F32)
    a3 = a - a1 - a2
    parts = (a1 + pltpu.roll(a2, 32, 1) + pltpu.roll(a3, 64, 1)).astype(BF16)
    tr = lax.broadcasted_iota(jnp.int32, (T, T), 0)
    tc = lax.broadcasted_iota(jnp.int32, (T, T), 1)
    tri = jnp.where(tc <= tr, 1.0, 0.0)
    tri_ch = jnp.where((tc <= tr) & ((tc >> 6) == (tr >> 6)), 1.0, 0.0)

    def collect(t):
        v = mm(t.astype(BF16), parts)
        v = v + pltpu.roll(v, 96, 1) + pltpu.roll(v, 64, 1)
        return jnp.where(lane < NH, v, 0.0)

    cum[...] = collect(tri_ch)
    cumd[...] = collect(tri)
    for c in range(NC):
        rc = pl.ds(c * CH, CH)
        cu = cum[rc, :]
        mid = cum[pl.ds(c * CH + CH // 2 - 1, 1), :]
        end = cum[pl.ds(c * CH + CH - 1, 1), :]
        uhl[rc, :] = split_rows(jnp.exp(cu - mid))
        through = jnp.where(start[pl.ds(c * CH + CH - 1, 1), :] < first_row + c * CH, 1.0, 0.0)
        rows_sc[pl.ds(c, 1), :] = jnp.exp(mid)
        rows_sc[pl.ds(8 + c, 1), :] = jnp.exp(end - mid)
        rows_sc[pl.ds(16 + c, 1), :] = jnp.exp(end) * through
        cum[rc, :] = step[c * CH : (c + 1) * CH] * jnp.exp(mid - cu)
    open_dev = jnp.where(start[pl.ds(T - 1, 1), :] < first_row, 1.0, 0.0)
    rows_sc[pl.ds(24, 1), :] = jnp.exp(cumd[pl.ds(T - 1, 1), :]) * open_dev
    ehl[...] = split_rows(jnp.where(start[...] < first_row, jnp.exp(cumd[...]), 0.0))
    rex[...] = mm(split_rows(rows_sc[pl.ds(0, 32), :]), ex[...])
    svhl = split_rows(cum[...])

    pl.semaphore_wait(barrier, 12)
    halo_x.start()
    halo_bc.start()
    for copy in exchange[0]:
        copy.start()

    loads[0].wait()
    loads[1].wait()
    xb[pl.ds(0, HALO), :] = jnp.zeros((HALO, INNER), BF16)
    bcb[pl.ds(0, HALO), :] = jnp.zeros((HALO, 512), BF16)
    split = jnp.swapaxes(bc3[...], 0, 1)
    bcb[pl.ds(HALO, T), pl.ds(0, 256)] = split[0]
    bcb[pl.ds(HALO, T), pl.ds(256, 256)] = split[1]
    taps_bc = jnp.swapaxes(cbc_ref[...], 0, 1).astype(F32)
    cbc[:, pl.ds(0, 256)] = taps_bc[0]
    cbc[:, pl.ds(256, 256)] = taps_bc[1]

    def convolve(src, cols, weight, cf):
        cf[...] = src[:, cols].astype(F32)
        out = cf[pl.ds(HALO, T), :] * weight[3:4]
        for lag in (1, 2, 3):
            out = out + cf[pl.ds(HALO - lag, T), :] * masks[lag - 1] * weight[3 - lag : 4 - lag]
        return silu(out).astype(BF16)

    def conv_bc(n, carry):
        cols = pl.ds(pl.multiple_of(n * 128, 128), 128)
        out = convolve(bcb, cols, cbc[:, cols], cf0)

        @pl.when(n < 2)
        def _():
            bm[:, cols] = out

        @pl.when(n >= 2)
        def _():
            cc[:, pl.ds(pl.multiple_of(n * 128 - 256, 128), 128)] = out
        return carry

    lax.fori_loop(0, 4, conv_bc, 0)

    def conv_quarter(o):
        def body(g, carry):
            first = g * GC + right[o] * NQ
            both_cols = pl.ds(pl.multiple_of(first, NQ), NQ)
            out = []
            for k, cf in enumerate((cf0, cf1)):
                cols = pl.ds(pl.multiple_of(first + k * 128, 128), 128)
                out.append(convolve(xb, cols, cx_ref[:, cols].astype(F32), cf))
                xc[:, cols] = out[-1]
            scale = mm(svhl, ex[:, both_cols])
            for k in (0, 1):
                cols = pl.ds(pl.multiple_of(first + k * 128, 128), 128)
                scaled = (out[k].astype(F32) * scale[:, k * 128 : (k + 1) * 128]).astype(BF16)
                for c in range(NC):
                    xh[c, pl.ds(ST, CH), cols] = scaled[c * CH : (c + 1) * CH]
            return carry

        lax.fori_loop(0, 2, body, 0)

    order = (2, 1, 3, 0)

    conv_quarter(order[0])
    conv_quarter(order[1])

    loads[5].wait()
    for copy in exchange[0]:
        copy.wait_recv()
    pair = jnp.swapaxes(kv3[...], 0, 1)
    kvb[0, :, pl.ds(0, 128)] = pair[1]
    kvb[0, :, pl.ds(128, 128)] = pair[0]
    kv_own()
    share_slot(0)
    for copy in exchange[1]:
        copy.start()

    halo_x.wait_recv()
    halo_bc.wait_recv()

    def first_rows(halo, own, weight):
        width = own.shape[1]
        v = jnp.concatenate([halo, own], 0).astype(F32)
        out = v[HALO:] * weight[3:4]
        for lag in (1, 2, 3):
            mask = jnp.concatenate([masks[lag - 1, pl.ds(0, HALO), :]] * (width // 128), 1)
            out = out + pltpu.roll(v, lag, 0)[HALO:] * mask * weight[3 - lag : 4 - lag]
        return silu(out).astype(BF16)

    halo_pair = jnp.swapaxes(hb3[...], 0, 1)
    head_rows, own_rows = pl.ds(0, HALO), pl.ds(HALO, HALO)
    bm[head_rows, :] = first_rows(halo_pair[0], bcb[own_rows, pl.ds(0, 256)], cbc[:, pl.ds(0, 256)])
    cc[head_rows, :] = first_rows(halo_pair[1], bcb[own_rows, pl.ds(256, 256)], cbc[:, pl.ds(256, 256)])
    for n in range(4):
        cols = pl.ds(n * 512, 512)
        out = first_rows(hx[:, cols], xb[own_rows, cols], cx_ref[:, cols].astype(F32))
        fixed[:, cols] = out
        fixed_s[:, cols] = (out.astype(F32) * mm(svhl[:HALO], ex[:, cols])).astype(BF16)

    out_c = pltpu.make_async_copy(cc, cc_ref, out_s.at[3])
    out_c.start()

    for c in range(NC):
        last = start[pl.ds(c * CH + CH - 1, 1), :]
        reach = pos[c * CH : (c + 1) * CH] >= last
        for g in (0, 1):
            b = jnp.where(reach, bm[pl.ds(c * CH, CH), pl.ds(g * 128, 128)].astype(F32), 0.0)
            bt[g, c] = jnp.transpose(b).astype(BF16)

    def end_states(o):
        quarter = right[o]

        def body(g, carry):
            cols = pl.ds(pl.multiple_of(g * GC + quarter * NQ, NQ), NQ)
            xc[head_rows, cols] = fixed[:, cols]
            xh[0, pl.ds(ST, HALO), cols] = fixed_s[:, cols]
            state = None
            for c in range(NC):
                if c == 0:
                    xh[c, pl.ds(0, ST), cols] = jnp.zeros((ST, NQ), BF16)
                else:
                    xh[c, pl.ds(0, ST), cols] = (state * rex[pl.ds(c, 1), cols]).astype(BF16)
                new = mm(bt[g, c], xh[c, pl.ds(ST, CH), cols])
                new = new * rex[pl.ds(8 + c, 1), cols]
                state = new if c == 0 else state * rex[pl.ds(16 + c, 1), cols] + new
            sdev[g, quarter, pl.ds(0, ST), :] = state.astype(BF16)
            d = jnp.broadcast_to(rex[pl.ds(24, 1), cols], (8, NQ))
            high = d.astype(BF16).astype(F32)
            sdev[g, quarter, pl.ds(ST, 16), :] = jnp.concatenate([high, d - high], 0).astype(BF16)
            return carry

        lax.fori_loop(0, 2, body, 0)

    def swap(o):
        return remote(
            sdev.at[1 - core, right[o]], srecv.at[right[o]], sx_s.at[o], sx_r.at[o], sibling)

    def decay_of(ref):
        d = ref[pl.ds(ST, 16), :].astype(F32)
        return d[0:1] + d[8:9]

    def both(quarter):
        mine, other = sdev.at[core, quarter], srecv.at[quarter]
        sm, so = mine[pl.ds(0, ST), :].astype(F32), other[pl.ds(0, ST), :].astype(F32)
        dm, do = decay_of(mine), decay_of(other)
        first = core == 0
        return (jnp.where(first, sm, so), jnp.where(first, dm, do), jnp.where(first, so, sm), jnp.where(first, do, dm))

    def deal(o):
        copies = [remote(sq.at[right[o]], got.at[1, x], st_s.at[3 + o], st_r.at[3 + o], at(z_next, right[o], core))]
        if o:
            copies.append(
                remote(sq.at[right[o]], got.at[0, x], st_s.at[o - 1], st_r.at[o - 1], at(z, right[o], core)))
        return copies

    def chip_state(o):
        quarter = right[o]
        swap(o).wait_recv()
        s0, d0, s1, d1 = both(quarter)
        sq[quarter, pl.ds(0, ST), :] = (s0 * d1 + s1).astype(BF16)
        d = jnp.broadcast_to(d0 * d1, (8, NQ))
        high = d.astype(BF16).astype(F32)
        sq[quarter, pl.ds(ST, 16), :] = jnp.concatenate([high, d - high], 0).astype(BF16)
        for copy in deal(o):
            copy.start()

    end_states(order[0])
    swap(order[0]).start()
    end_states(order[1])
    swap(order[1]).start()
    chip_state(order[0])

    for k in (2, 3):
        conv_quarter(order[k])
        chip_state(order[k - 1])
        end_states(order[k])
        swap(order[k]).start()

    for d in range(9):
        block = lax.rem(s + BLOCKS - d, BLOCKS)
        key = row + block * T
        hot = (key >= doc_first) & (key < doc_end)
        kvb[d, :, pl.ds(256, 128)] = jnp.where(hot, 1.0, 0.0).astype(BF16)
        if d == 0:
            blind = jnp.where(hot | (lane >= DOCS), 0.0, MASKED).astype(BF16)
            for i in range(QH):
                qa[i, :, pl.ds(128, 128)] = blind

    loads[4].wait()
    for copy in exchange[1]:
        copy.wait_recv()
    for i in range(QH):
        qa[i, :, pl.ds(0, 128)] = qb[:, pl.ds(i * 128, 128)]

    chip_state(order[3])
    kv_risen(0)
    got[0, x] = sq[x]

    RT = 128
    scs, pbs, ars = (sc0, sc1), (pb0, pb1), (ar0, ar1)

    def attend(slots, first):
        tiles = T * len(slots) // 128

        def scores(i):
            for n, d in enumerate(slots):
                scs[i % 2][:, pl.ds(n * T, T)] = mm_nt(qa[i], kvb[d, :, pl.ds(128, 256)])

        def block(i, r, k):
            v = scs[i % 2][pl.ds(r * RT, RT), pl.ds(k * 128, 128)]
            if first and k == r:
                rr = lax.broadcasted_iota(jnp.int32, (RT, 128), 0)
                cc_ = lax.broadcasted_iota(jnp.int32, (RT, 128), 1)
                v = jnp.where(cc_ <= rr, v, MASKED)
            return v

        def highest(i, r):
            rs = pl.ds(r * RT, RT)
            top = block(i, r, 0)
            for k in range(1, r + 1 if first else tiles):
                top = jnp.maximum(top, block(i, r, k))
            top = jnp.max(top, axis=1, keepdims=True)
            if first:
                mrow[i, rs, :] = jnp.broadcast_to(top, (RT, 128))
            else:
                old = mrow[i, rs, :]
                new = jnp.maximum(old, top)
                ars[i % 2][rs, :] = jnp.exp2((old - new) * SCORE)
                mrow[i, rs, :] = new

        def weigh(i, r):
            rs = pl.ds(r * RT, RT)
            new, part = mrow[i, rs, :], None
            for k in range(tiles):
                if first and k > r:
                    pbs[i % 2][rs, pl.ds(k * 128, 128)] = jnp.zeros((RT, 128), BF16)
                    continue
                p = jnp.exp2((block(i, r, k) - new) * SCORE)
                part = p if part is None else part + p
                pbs[i % 2][rs, pl.ds(k * 128, 128)] = p.astype(BF16)
            lrow[i, rs, :] = part if first else lrow[i, rs, :] * ars[i % 2][rs, :] + part

        def gather(i):
            out = mm(pbs[i % 2][:, pl.ds(0, T)], kvb[slots[0], :, pl.ds(0, 128)])
            for n, d in enumerate(slots[1:]):
                out = out + mm(pbs[i % 2][:, pl.ds((n + 1) * T, T)], kvb[d, :, pl.ds(0, 128)])
            acc[i] = out if first else acc[i] * ars[i % 2][...] + out

        scores(0)
        for i in range(QH):
            if i + 1 < QH:
                scores(i + 1)
            if i > 0:
                gather(i - 1)
            for r in range(T // RT):
                highest(i, r)
            for r in range(T // RT):
                weigh(i, r)
        gather(QH - 1)

    attend((0,), True)

    loads[3].wait()

    for c in range(NC):
        rc = pl.ds(c * CH, CH)
        begin = start[rc, :]
        base = first_row + c * CH
        tpos = lax.broadcasted_iota(jnp.int32, (CH, CH), 0)
        spos = lax.broadcasted_iota(jnp.int32, (CH, CH), 1)
        for g in (0, 1):
            gl = pl.ds(g * 128, 128)
            cg = cc[rc, gl]
            grid = mm_nt(cg, bm[rc, gl])
            grid = jnp.where((spos <= tpos) & (spos + base >= begin[:, :CH]), grid, 0.0).astype(BF16)
            mix[g, c, :, pl.ds(0, 128)] = jnp.where(begin < base, cg.astype(F32), 0.0).astype(BF16)
            mix[g, c, :, pl.ds(128, CH)] = grid

    def local(n, carry):
        g = n >> 2
        cols = pl.ds(pl.multiple_of(n * 256, 256), 256)
        ue[...] = mm(uhl[...], ex[:, cols])
        ee[...] = mm(ehl[...], ex[:, cols])
        for c in range(NC):
            rc = pl.ds(c * CH, CH)
            y = mm(mix[g, c], xh[c, :, cols])
            y = y * ue[rc, :] + rex[pl.ds(25, 1), cols] * xc[rc, cols].astype(F32)
            sg = silu(gb[rc, cols].astype(F32))
            yg[rc, cols] = (y * sg).astype(BF16)
            eg[rc, cols] = (ee[rc, :] * sg).astype(BF16)
        pltpu.make_async_copy(yg.at[:, cols], yg_ref.at[:, cols], out_s.at[1]).start()
        pltpu.make_async_copy(eg.at[:, cols], eg_ref.at[:, cols], out_s.at[2]).start()
        return carry

    def locals_(lo, hi):
        lax.fori_loop(lo, hi, local, 0)

    kv_risen(1)
    share_slot(8)
    locals_(0, 4)
    shared(8)
    attend((8, 7 - 6 * core), False)

    for o in order:
        for copy in deal(o):
            copy.wait_recv()

    def decay(r, j):
        d = got[r, j, pl.ds(ST, 16), :].astype(F32)
        return d[0:1] + d[8:9]

    def entering(n, carry):
        rs = pl.ds(pl.multiple_of(n * 32, 32), 32)
        later, fall = [None] * 4, None
        for j in (3, 2, 1, 0):
            v = got[1, j, rs, :].astype(F32)
            later[j] = v if j == 3 else later[j + 1] + fall * v
            fall = decay(1, j) if j == 3 else fall * decay(1, j)
        tq[0, rs, :] = later[0].astype(BF16)
        for j in (0, 1, 2):
            v = got[0, j, rs, :].astype(F32)
            row_sum = v if j == 0 else v + decay(0, j) * row_sum
            fall = decay(0, j) if j == 0 else fall * decay(0, j)
            tq[j + 1, rs, :] = (row_sum + fall * later[j + 1]).astype(BF16)
        return carry

    lax.fori_loop(0, ST // 32, entering, 0)
    back = [
        remote(tq.at[right[o]], tback.at[x], tq_s.at[o - 1], tq_r.at[o - 1], at(z, right[o], core)) for o in (1, 2, 3)
    ]
    for copy in back:
        copy.start()
    tback[x] = tq[x]

    locals_(4, 6)
    for o in (1, 2, 3):
        kv_row(o)
        share_slot(2 * o)
    locals_(6, 8)
    shared(2)
    shared(4)
    attend((2, 1 + 2 * core, 4, 3 + 2 * core), False)
    for copy in back:
        copy.wait_recv()

    def enter(n, carry):
        cols = pl.ds(pl.multiple_of(n * NQ, NQ), NQ)
        t = tback[n].astype(F32)
        s0, d0, _, _ = both(n)
        t1 = s0 + d0 * t
        first = core == 0
        tin[core, :, cols] = jnp.where(first, t, t1).astype(BF16)
        give_b[:, cols] = jnp.where(first, t1, t).astype(BF16)
        return carry

    lax.fori_loop(0, 4, enter, 0)
    give = remote(give_b, tin.at[core], tx_s, tx_r, sibling)
    give.start()
    shared(6)
    attend((6, 5 + 2 * core), False)

    def finish_head(i, carry):
        total = jnp.sum(lrow[i], axis=1, keepdims=True)
        ab[:, pl.ds(pl.multiple_of(i * 128, 128), 128)] = (acc[i] / total).astype(BF16)
        return carry

    lax.fori_loop(0, QH, finish_head, 0)
    out_a = pltpu.make_async_copy(ab, ao_ref, out_s.at[0])
    out_a.start()

    remote(give_b, tin.at[1 - core], tx_s, tx_r, sibling).wait_recv()

    out_t = pltpu.make_async_copy(tin, tin_ref, out_s.at[4])
    out_t.start()

    for group in exchange:
        for copy in group:
            copy.wait_send()
    halo_x.wait_send()
    halo_bc.wait_send()
    for i in (0, 1):
        rise[i].wait_send()
        for o in (1, 2, 3):
            along(o, i, 0).wait_send()
    for o in order:
        swap(o).wait_send()
        for copy in deal(o):
            copy.wait_send()
    for copy in back:
        copy.wait_send()
    for i in range(4):
        share(i).wait_send()
    give.wait_send()
    out_a.wait()
    pltpu.make_async_copy(yg, yg_ref, out_s.at[1]).wait()
    pltpu.make_async_copy(eg, eg_ref, out_s.at[2]).wait()
    out_c.wait()
    out_t.wait()

TR = 128
SUB = 16


def finish(yg_ref, eg_ref, cc_ref, tin_ref, gain_ref, a_ref, mo_ref, ao_ref, yg, eg, cc, tin, ab, far, ob, in_s, row_s, out_s):
    small = [pltpu.make_async_copy(tin_ref, tin, in_s.at[0]), pltpu.make_async_copy(cc_ref, cc, in_s.at[1])]
    large = []
    for i in range(T // TR):
        r = pl.ds(i * TR, TR)
        large.append((
            pltpu.make_async_copy(yg_ref.at[r], yg.at[r], row_s.at[0, i]),
            pltpu.make_async_copy(eg_ref.at[r], eg.at[r], row_s.at[1, i])))
    came = pltpu.make_async_copy(a_ref, ab, in_s.at[2])
    for copy in small + [copy for pair in large for copy in pair] + [came]:
        copy.start()
    for copy in small:
        copy.wait()
    attention = pltpu.make_async_copy(ab, ao_ref, out_s.at[T // TR])
    outs = [attention]
    for i in range(T // TR):
        r = pl.ds(i * TR, TR)
        for copy in large[i]:
            copy.wait()
        for g in range(2):
            cols = pl.ds(g * GC, GC)
            gain = gain_ref[cols].reshape(1, GC)
            far[r, cols] = mm(cc[r, pl.ds(g * 128, 128)], tin[g])
            for k in range(TR // SUB):
                q = pl.ds(i * TR + k * SUB, SUB)
                gated = yg[q, cols].astype(F32) + eg[q, cols].astype(F32) * far[q, cols]
                mean = jnp.sum(gated * gated, axis=1, keepdims=True) * (1.0 / GC)
                scale = lax.rsqrt(mean + EPSILON)
                ob[q, cols] = (gated * scale * gain).astype(BF16)
        outs.append(pltpu.make_async_copy(ob.at[r], mo_ref.at[r], out_s.at[i]))
        outs[-1].start()
    came.wait()
    attention.start()
    for copy in outs:
        copy.wait()


def per_device(
    x_in, bc_in, gate_in, step_size, decay_rate, skip, conv_x, conv_bc, norm_gain, queries, keys_values, doc_lengths
):
    vm, hbm = pl.BlockSpec(memory_space=pltpu.VMEM), pl.BlockSpec(memory_space=pltpu.HBM)
    dma = pltpu.SemaphoreType.DMA
    V = pltpu.VMEM
    shape = jax.ShapeDtypeStruct
    main = pl.pallas_call(
        kernel,
        out_shape=(
            shape((T, INNER), BF16), shape((T, INNER), BF16), shape((T, 256), BF16),
            shape((2, ST, GC), BF16), shape((T, QH * AD), BF16),
        ),
        in_specs=[pl.BlockSpec(memory_space=pltpu.SMEM)] + [vm] * 4 + [hbm] * 6,
        out_specs=(hbm,) * 5,
        scratch_shapes=[
            V((HALO + T, INNER), BF16),
            V((HALO, INNER), BF16),
            V((T, 2, 256), BF16),
            V((HALO, 2, 256), BF16),
            V((HALO + T, 512), BF16),
            V((4, 512), F32),
            V((T, INNER), BF16),
            V((128, T), F32),
            V((T, 512), BF16),
            V((QH, T, 256), BF16),
            V((T, 2, 128), BF16),
            V((9, T, 384), BF16),
            V((HALO + T, 128), F32),
            V((HALO + T, 128), F32),
            V((T, 128), jnp.int32),
            V((3, T, 128), F32),
            V((T, INNER), BF16),
            V((NC, ST + CH, INNER), BF16),
            V((HALO, INNER), BF16),
            V((HALO, INNER), BF16),
            V((T, 256), BF16),
            V((2, NC, ST, CH), BF16),
            V((2, NC, CH, ST + CH), BF16),
            V((128, INNER), BF16),
            V((T, 128), F32),
            V((T, 128), F32),
            V((2, 4, ST + 16, NQ), BF16),
            V((4, ST + 16, NQ), BF16),
            V((4, ST + 16, NQ), BF16),
            V((2, 4, ST + 16, NQ), BF16),
            V((4, ST, NQ), BF16),
            V((4, ST, NQ), BF16),
            V((ST, GC), BF16),
            V((2, ST, GC), BF16),
            V((T, 128), BF16),
            V((T, 128), BF16),
            V((40, 128), F32),
            V((32, INNER), F32),
            V((T, 256), F32),
            V((T, 256), F32),
            V((T, INNER), BF16),
            V((T, INNER), BF16),
            V((T, 256), BF16),
            V((T, 512), BF16),
            V((T, 4 * T), F32),
            V((T, 4 * T), F32),
            V((T, 4 * T), BF16),
            V((T, 4 * T), BF16),
            V((QH, T, 128), F32),
            V((QH, T, 128), F32),
            V((T, 128), F32),
            V((T, 128), F32),
            V((QH, T, 128), F32),
            dma((6,)),
            dma((2, 3)),
            dma((2, 3)),
            dma((2,)),
            dma((2,)),
            dma((2,)),
            dma((2,)),
            dma((3, 2)),
            dma((3, 2)),
            dma((4,)),
            dma((4,)),
            dma((7,)),
            dma((7,)),
            dma((3,)),
            dma((3,)),
            dma((4,)),
            dma((4,)),
            dma,
            dma,
            dma((5,)),
        ],
        compiler_params=pltpu.CompilerParams(
            collective_id=0, has_side_effects=True, vmem_limit_bytes=60 * 1024 * 1024
        ),
        name="hybrid",
    )
    yg, eg, cc, tin, attended = main(
        doc_lengths, decay_rate, skip, conv_x, conv_bc, x_in, bc_in, gate_in, step_size.T, queries, keys_values)
    return pl.pallas_call(
        finish,
        out_shape=(shape((T, INNER), BF16), shape((T, QH * AD), BF16)),
        in_specs=[hbm] * 4 + [vm, hbm],
        out_specs=(hbm, hbm),
        scratch_shapes=[
            V((T, INNER), BF16), V((T, INNER), BF16), V((T, 256), BF16), V((2, ST, GC), BF16), V((T, QH * AD), BF16),
            V((T, INNER), F32), V((T, INNER), BF16), dma((3,)), dma((2, T // TR)), dma((T // TR + 1,)),
        ],
        compiler_params=pltpu.CompilerParams(vmem_limit_bytes=60 * 1024 * 1024),
        name="finish",
    )(yg, eg, cc, tin, norm_gain, attended)


def solution(mesh):
    placed = (
        P("seq", "head"),
        P("seq", None, "head"),
        P("seq", "head"),
        P("seq", "head"),
        P("head"),
        P("head"),
        P(None, "head"),
        P(None, None, "head"),
        P("head"),
        P(("seq", "head"), None),
        P(("seq", "head"), None, None),
        P(),
    )
    return jax.shard_map(
        per_device,
        mesh=mesh,
        in_specs=placed,
        out_specs=(P("seq", "head"), P("seq", "head")),
        check_vma=False,
    )
```

time: 56.4 us -> 51.2 us (0.908)
  the two profiles are of different devices: /device:TPU:97 before, /device:TPU:1 now
where the time goes in v2:
time: 51.2 us; the launch traced here: 51 us
  Pallas kernels  50.2 us (98%)
  between operations  0.8 us (2%)
    pallas_call x1, Pallas kernels, per_device(): main(doc_lengths, decay_rate, skip, conv_x, conv_bc, x_in, bc_in, gate_in...  45.3 us
    pallas_call x1, Pallas kernels, per_device(): pl.pallas_call(finish, out_shape=(shape((T, INNER), BF16), shape((T, QH *...  4.87 us

profile of v2, /device:TPU:1, one launch (start us, length us, event | category | flops | bytes accessed | tf_op | source)
XLA Modules:
  0.0 51.0 jit_solution(17322636418416734407)
XLA Ops:
  0.6 45.3 %hybrid.1 = (bf16[384,2048]{1,0:T(8,128)(2,1)}, bf16[384,2048]{1,0:T(8,128)(2,1)}, bf16[384,256]{1,0:T(8,128)(2,1)}, bf16[2,128,1024]{2,1,0:T(8,128)(2,1)}, bf16[384,512]{1,0:T(8,128)(2,1)}) custom-call(s32[16]{0:T(128)} %dl_ref.1, f32[32]{0:T(128)} %dec_ref.1, f32[32]{0:T(128)} %skip_ref.1, bf16[4,2048]{1,0:T(4,128)(2,1)} %cx_ref.1, ...), custom_call_target="tpu_custom_call" | custom-call | tf_op jit(solution)/shard_map/hybrid/pallas_call | solution.py:779
  46.0 4.9 %finish.1 = (bf16[384,2048]{1,0:T(8,128)(2,1)}, bf16[384,512]{1,0:T(8,128)(2,1)}) custom-call(bf16[384,2048]{1,0:T(8,128)(2,1)} %get-tuple-element.7.yg_ref, bf16[384,2048]{1,0:T(8,128)(2,1)} %get-tuple-element.8.eg_ref, bf16[384,256]{1,0:T(8,128)(2,1)} %get-tuple-element.9.cc_ref, bf16[2,128,1024]{2,1,0:T(8,128)(2,1)} %get-tuple-element.10.tin_ref, ...), custom_call_target="tpu_custom_call" | custom-call | tf_op jit(solution)/shard_map/finish/pallas_call | solution.py:781

commit v3 on v2

--- a/solution.py
+++ b/solution.py
@@ -53,7 +53,7 @@
     dl_ref, dec_ref, skip_ref, cx_ref, cbc_ref,
     x_ref, bc_ref, gate_ref, step_ref, q_ref, kv_ref,
     yg_ref, eg_ref, cc_ref, tin_ref, ao_ref,
-    xb, hx, bc3, hb3, bcb, cbc, gb, stt, qb, qa, kv3, kvb, cf0, cf1, start, masks, xc, xh, fixed, fixed_s, bm, bt, mix, ex, cum, cumd, sdev, srecv, sq, got, tq, tback, give_b, tin,
+    xb, hx, bc3, hb3, bcb, cbc, gb, stt, qb, qa, kv3, kv3z, kvb, cf0, cf1, start, masks, xc, xh, fixed, fixed_s, bm, bt, mix, ex, cum, cumd, sdev, srecv, sq, got, tq, tback, give_b, tin,
     uhl, ehl, rows_sc, rex, ue, ee, yg, eg, cc, ab, sc0, sc1, pb0, pb1, mrow, lrow, ar0, ar1, acc,
     loc_s, a_s, a_r, halo_s, halo_r, z_s, z_r, row_s, row_r, sh_s, sh_r, st_s, st_r, tq_s, tq_r,
     sx_s, sx_r, tx_s, tx_r, out_s,
@@ -109,6 +109,9 @@
         pl.semaphore_signal(barrier, inc=1, device_id=at(z, left[o], core), device_id_type=MESH)
     for o in (0, 1, 2, 3):
         pl.semaphore_signal(barrier, inc=1, device_id=at(z_prev, left[o], core), device_id_type=MESH)
+    for o in (1, 2, 3):
+        pl.semaphore_signal(
+            barrier, inc=1, device_id={"seq": (z_prev * 4 + x) * 2 + core, "head": peer(o)}, device_id_type=MESH)
 
     def a2a(o, which):
         to = peer(o)
@@ -129,25 +132,41 @@
     def block_half(d, i):
         return kvb.at[d, pl.ds(i * HT, HT), pl.ds(0, 256)]
 
-    rise = [remote(block_half(0, i), block_half(8, i), z_s.at[i], z_r.at[i], above) for i in (0, 1)]
+    def rising(o):
+        to = peer(o)
+        return remote(
+            kv_ref.at[:, :, pl.ds(pl.multiple_of(to * 128, 128), 128)], kv3z.at[pl.ds(pl.multiple_of(h * 96, 32), 96)],
+            z_s.at[o], z_r.at[o], {"seq": (z_next * 4 + x) * 2 + core, "head": to})
+
+    rise = [rising(o) for o in (0, 1, 2, 3)]
 
     def along(o, i, source):
         return remote(
             block_half(source, i), block_half(2 * o, i), row_s.at[o - 1, i], row_r.at[o - 1, i], at(z, right[o], core))
 
+    def unpack(buffer, d):
+        pair = jnp.swapaxes(buffer[...], 0, 1)
+        kvb[d, :, pl.ds(0, 128)] = pair[1]
+        kvb[d, :, pl.ds(128, 128)] = pair[0]
+
     def kv_own():
+        loads[5].wait()
+        for copy in exchange[0]:
+            copy.wait_recv()
+        unpack(kv3, 0)
+        for i in (0, 1):
+            for o in (1, 2, 3):
+                pl.when(x + o < 4)(along(o, i, 0).start)
+        share_slot(0)
+
+    def kv_risen():
         for copy in rise:
-            copy.start()
-        for o in (1, 2, 3):
-            @pl.when(x + o < 4)
-            def _():
-                for i in (0, 1):
-                    along(o, i, 0).start()
-
-    def kv_risen(i):
-        rise[i].wait_recv()
-        for o in (3, 2, 1):
-            pl.when(x + o >= 4)(along(o, i, 8).start)
+            copy.wait_recv()
+        unpack(kv3z, 8)
+        for i in (0, 1):
+            for o in (3, 2, 1):
+                pl.when(x + o >= 4)(along(o, i, 8).start)
+        share_slot(8)
 
     def kv_row(o):
         for i in (0, 1):
@@ -244,10 +263,10 @@
     rex[...] = mm(split_rows(rows_sc[pl.ds(0, 32), :]), ex[...])
     svhl = split_rows(cum[...])
 
-    pl.semaphore_wait(barrier, 12)
+    pl.semaphore_wait(barrier, 15)
     halo_x.start()
     halo_bc.start()
-    for copy in exchange[0]:
+    for copy in exchange[0] + rise:
         copy.start()
 
     loads[0].wait()
@@ -307,16 +326,8 @@
     conv_quarter(order[0])
     conv_quarter(order[1])
 
-    loads[5].wait()
-    for copy in exchange[0]:
-        copy.wait_recv()
-    pair = jnp.swapaxes(kv3[...], 0, 1)
-    kvb[0, :, pl.ds(0, 128)] = pair[1]
-    kvb[0, :, pl.ds(128, 128)] = pair[0]
-    kv_own()
-    share_slot(0)
-    for copy in exchange[1]:
-        copy.start()
+    conv_quarter(order[2])
+    conv_quarter(order[3])
 
     halo_x.wait_recv()
     halo_bc.wait_recv()
@@ -389,12 +400,11 @@
         first = core == 0
         return (jnp.where(first, sm, so), jnp.where(first, dm, do), jnp.where(first, so, sm), jnp.where(first, do, dm))
 
-    def deal(o):
-        copies = [remote(sq.at[right[o]], got.at[1, x], st_s.at[3 + o], st_r.at[3 + o], at(z_next, right[o], core))]
-        if o:
-            copies.append(
-                remote(sq.at[right[o]], got.at[0, x], st_s.at[o - 1], st_r.at[o - 1], at(z, right[o], core)))
-        return copies
+    def deal_up(o):
+        return remote(sq.at[right[o]], got.at[1, x], st_s.at[3 + o], st_r.at[3 + o], at(z_next, right[o], core))
+
+    def deal_row(o):
+        return remote(sq.at[right[o]], got.at[0, x], st_s.at[o - 1], st_r.at[o - 1], at(z, right[o], core))
 
     def chip_state(o):
         quarter = right[o]
@@ -404,20 +414,26 @@
         d = jnp.broadcast_to(d0 * d1, (8, NQ))
         high = d.astype(BF16).astype(F32)
         sq[quarter, pl.ds(ST, 16), :] = jnp.concatenate([high, d - high], 0).astype(BF16)
-        for copy in deal(o):
-            copy.start()
-
+        deal_up(o).start()
+        if o:
+            pl.when(x < 3)(deal_row(o).start)
+
+    kv_own()
+    for copy in exchange[1]:
+        copy.start()
     end_states(order[0])
     swap(order[0]).start()
     end_states(order[1])
     swap(order[1]).start()
     chip_state(order[0])
-
-    for k in (2, 3):
-        conv_quarter(order[k])
-        chip_state(order[k - 1])
-        end_states(order[k])
-        swap(order[k]).start()
+    end_states(order[2])
+    swap(order[2]).start()
+    chip_state(order[1])
+    kv_risen()
+    end_states(order[3])
+    swap(order[3]).start()
+    chip_state(order[2])
+    chip_state(order[3])
 
     for d in range(9):
         block = lax.rem(s + BLOCKS - d, BLOCKS)
@@ -435,8 +451,6 @@
     for i in range(QH):
         qa[i, :, pl.ds(0, 128)] = qb[:, pl.ds(i * 128, 128)]
 
-    chip_state(order[3])
-    kv_risen(0)
     got[0, x] = sq[x]
 
     RT = 128
@@ -538,15 +552,14 @@
     def locals_(lo, hi):
         lax.fori_loop(lo, hi, local, 0)
 
-    kv_risen(1)
-    share_slot(8)
     locals_(0, 4)
     shared(8)
     attend((8, 7 - 6 * core), False)
 
     for o in order:
-        for copy in deal(o):
-            copy.wait_recv()
+        deal_up(o).wait_recv()
+        if o:
+            pl.when(left[o] < 3)(deal_row(o).wait_recv)
 
     def decay(r, j):
         d = got[r, j, pl.ds(ST, 16), :].astype(F32)
@@ -621,14 +634,16 @@
             copy.wait_send()
     halo_x.wait_send()
     halo_bc.wait_send()
+    for copy in rise:
+        copy.wait_send()
     for i in (0, 1):
-        rise[i].wait_send()
         for o in (1, 2, 3):
             along(o, i, 0).wait_send()
     for o in order:
         swap(o).wait_send()
-        for copy in deal(o):
-            copy.wait_send()
+        deal_up(o).wait_send()
+        if o:
+            pl.when(x < 3)(deal_row(o).wait_send)
     for copy in back:
         copy.wait_send()
     for i in range(4):
@@ -707,6 +722,7 @@
             V((128, T), F32),
             V((T, 512), BF16),
             V((QH, T, 256), BF16),
+            V((T, 2, 128), BF16),
             V((T, 2, 128), BF16),
             V((9, T, 384), BF16),
             V((HALO + T, 128), F32),
@@ -755,8 +771,8 @@
             dma((2, 3)),
             dma((2,)),
             dma((2,)),
-            dma((2,)),
-            dma((2,)),
+            dma((4,)),
+            dma((4,)),
             dma((3, 2)),
             dma((3, 2)),
             dma((4,)),

time: 51.2 us -> 50.1 us (0.979)
  Pallas kernels: 50.2 us -> 49 us
    pallas_call x1, Pallas kernels: 45.3 us -> 44.1 us  [per_device(): main(doc_lengths, decay_rate, skip, conv_x, conv_bc, x_in, bc_in, gate_in...]
where the time goes in v3:
time: 50.1 us; the launch traced here: 49.8 us
  Pallas kernels  49 us (98%)
  between operations  0.8 us (2%)
    pallas_call x1, Pallas kernels, per_device(): main(doc_lengths, decay_rate, skip, conv_x, conv_bc, x_in, bc_in, gate_in...  44.1 us
    pallas_call x1, Pallas kernels, per_device(): pl.pallas_call(finish, out_shape=(shape((T, INNER), BF16), shape((T, QH *...  4.87 us

profile of v3, /device:TPU:1, one launch (start us, length us, event | category | flops | bytes accessed | tf_op | source)
XLA Modules:
  0.0 49.8 jit_solution(11434972753463453094)
XLA Ops:
  0.6 44.1 %hybrid.1 = (bf16[384,2048]{1,0:T(8,128)(2,1)}, bf16[384,2048]{1,0:T(8,128)(2,1)}, bf16[384,256]{1,0:T(8,128)(2,1)}, bf16[2,128,1024]{2,1,0:T(8,128)(2,1)}, bf16[384,512]{1,0:T(8,128)(2,1)}) custom-call(s32[16]{0:T(128)} %dl_ref.1, f32[32]{0:T(128)} %dec_ref.1, f32[32]{0:T(128)} %skip_ref.1, bf16[4,2048]{1,0:T(4,128)(2,1)} %cx_ref.1, ...), custom_call_target="tpu_custom_call" | custom-call | tf_op jit(solution)/shard_map/hybrid/pallas_call | solution.py:795
  44.8 4.9 %finish.1 = (bf16[384,2048]{1,0:T(8,128)(2,1)}, bf16[384,512]{1,0:T(8,128)(2,1)}) custom-call(bf16[384,2048]{1,0:T(8,128)(2,1)} %get-tuple-element.7.yg_ref, bf16[384,2048]{1,0:T(8,128)(2,1)} %get-tuple-element.8.eg_ref, bf16[384,256]{1,0:T(8,128)(2,1)} %get-tuple-element.9.cc_ref, bf16[2,128,1024]{2,1,0:T(8,128)(2,1)} %get-tuple-element.10.tin_ref, ...), custom_call_target="tpu_custom_call" | custom-call | tf_op jit(solution)/shard_map/finish/pallas_call | solution.py:797

commit v4 on v3

--- a/solution.py
+++ b/solution.py
@@ -553,9 +553,6 @@
         lax.fori_loop(lo, hi, local, 0)
 
     locals_(0, 4)
-    shared(8)
-    attend((8, 7 - 6 * core), False)
-
     for o in order:
         deal_up(o).wait_recv()
         if o:
@@ -587,6 +584,9 @@
     for copy in back:
         copy.start()
     tback[x] = tq[x]
+
+    shared(8)
+    attend((8, 7 - 6 * core), False)
 
     locals_(4, 6)
     for o in (1, 2, 3):
@@ -672,7 +672,7 @@
         copy.start()
     for copy in small:
         copy.wait()
-    attention = pltpu.make_async_copy(ab, ao_ref, out_s.at[T // TR])
+    attention = pltpu.make_async_copy(ab, ao_ref, out_s.at[2 * (T // TR)])
     outs = [attention]
     for i in range(T // TR):
         r = pl.ds(i * TR, TR)
@@ -688,10 +688,11 @@
                 mean = jnp.sum(gated * gated, axis=1, keepdims=True) * (1.0 / GC)
                 scale = lax.rsqrt(mean + EPSILON)
                 ob[q, cols] = (gated * scale * gain).astype(BF16)
-        outs.append(pltpu.make_async_copy(ob.at[r], mo_ref.at[r], out_s.at[i]))
-        outs[-1].start()
-    came.wait()
-    attention.start()
+            outs.append(pltpu.make_async_copy(ob.at[r, cols], mo_ref.at[r, cols], out_s.at[2 * i + g]))
+            outs[-1].start()
+        if i == 0:
+            came.wait()
+            attention.start()
     for copy in outs:
         copy.wait()
 
@@ -801,7 +802,7 @@
         out_specs=(hbm, hbm),
         scratch_shapes=[
             V((T, INNER), BF16), V((T, INNER), BF16), V((T, 256), BF16), V((2, ST, GC), BF16), V((T, QH * AD), BF16),
-            V((T, INNER), F32), V((T, INNER), BF16), dma((3,)), dma((2, T // TR)), dma((T // TR + 1,)),
+            V((T, INNER), F32), V((T, INNER), BF16), dma((3,)), dma((2, T // TR)), dma((2 * (T // TR) + 1,)),
         ],
         compiler_params=pltpu.CompilerParams(vmem_limit_bytes=60 * 1024 * 1024),
         name="finish",

time: 50.1 us -> 52.3 us (1.044)
  the two profiles are of different devices: /device:TPU:1 before, /device:TPU:11 now
where the time goes in v4:
time: 52.3 us; the launch traced here: 52.1 us
  Pallas kernels  51.3 us (98%)
  between operations  0.8 us (2%)
    pallas_call x1, Pallas kernels, per_device(): main(doc_lengths, decay_rate, skip, conv_x, conv_bc, x_in, bc_in, gate_in...  46.6 us
    pallas_call x1, Pallas kernels, per_device(): pl.pallas_call(finish, out_shape=(shape((T, INNER), BF16), shape((T, QH *...  4.7 us

profile of v4, /device:TPU:11, one launch (start us, length us, event | category | flops | bytes accessed | tf_op | source)
XLA Modules:
  0.0 52.1 jit_solution(8445466132430267327)
XLA Ops:
  0.6 46.6 %hybrid.1 = (bf16[384,2048]{1,0:T(8,128)(2,1)}, bf16[384,2048]{1,0:T(8,128)(2,1)}, bf16[384,256]{1,0:T(8,128)(2,1)}, bf16[2,128,1024]{2,1,0:T(8,128)(2,1)}, bf16[384,512]{1,0:T(8,128)(2,1)}) custom-call(s32[16]{0:T(128)} %dl_ref.1, f32[32]{0:T(128)} %dec_ref.1, f32[32]{0:T(128)} %skip_ref.1, bf16[4,2048]{1,0:T(4,128)(2,1)} %cx_ref.1, ...), custom_call_target="tpu_custom_call" | custom-call | tf_op jit(solution)/shard_map/hybrid/pallas_call | solution.py:796
  47.2 4.7 %finish.1 = (bf16[384,2048]{1,0:T(8,128)(2,1)}, bf16[384,512]{1,0:T(8,128)(2,1)}) custom-call(bf16[384,2048]{1,0:T(8,128)(2,1)} %get-tuple-element.7.yg_ref, bf16[384,2048]{1,0:T(8,128)(2,1)} %get-tuple-element.8.eg_ref, bf16[384,256]{1,0:T(8,128)(2,1)} %get-tuple-element.9.cc_ref, bf16[2,128,1024]{2,1,0:T(8,128)(2,1)} %get-tuple-element.10.tin_ref, ...), custom_call_target="tpu_custom_call" | custom-call | tf_op jit(solution)/shard_map/finish/pallas_call | solution.py:798
